TPU v7x, 32 devices: a whole 2x2x4 slice. The times are simulated.
32 devices in a mesh: pop: 4 (over x, core), fsdp: 8 (over z, y).
Axes of the slice: x: 2, y: 2, z: 4, core: 2. Of those that a mesh axis runs over, the one named last changes fastest.
Arguments:
- tokens: bfloat16 [512, 5120], P('pop', 'fsdp'), may hold values from -6 to 6
- seeds: int32 [512], replicated, may hold values from 0 to 1048575
- fitness: float32 [512], P(('pop', 'fsdp')), may hold values from -60 to 60
- gate_weight: bfloat16 [5120, 14336], P('fsdp', 'pop'), may hold values from -0.078125 to 0.078125
- up_weight: bfloat16 [5120, 14336], P('fsdp', 'pop'), may hold values from -0.078125 to 0.078125
- gate_first: float32 [5120, 14336], P('fsdp', 'pop'), may hold values from -4 to 4
- up_first: float32 [5120, 14336], P('fsdp', 'pop'), may hold values from -4 to 4
- gate_second: float32 [5120, 14336], P('fsdp', 'pop'), may hold values from 0.05 to 2
- up_second: float32 [5120, 14336], P('fsdp', 'pop'), may hold values from 0.05 to 2
Outputs:
- hidden: bfloat16 [512, 14336], P('fsdp', 'pop')
- gate_new: bfloat16 [5120, 14336], P('fsdp', 'pop')
- up_new: bfloat16 [5120, 14336], P('fsdp', 'pop')
- gate_first_new: float32 [5120, 14336], P('fsdp', 'pop')
- up_first_new: float32 [5120, 14336], P('fsdp', 'pop')
- gate_second_new: float32 [5120, 14336], P('fsdp', 'pop')
- up_second_new: float32 [5120, 14336], P('fsdp', 'pop')
All inputs are finite; a program needn't handle non-finite values.
Results may differ from a plain program's by a relative error of at most 0.0022.
Values may be sent and summed in bfloat16 or wider, within the bound.
No kernel may reach another device: no remote copies, remote signals or barrier semaphores. Data moves between devices by JAX's collectives and lax.ppermute only.
A program may use at most 192 MiB of HBM per device.

v0:
```python
import jax
import jax.numpy as jnp
from jax import lax
from jax.sharding import PartitionSpec as P

noise_scale = 0.01
learn_rate = 0.002
beta_first = 0.9
beta_second = 0.99
adam_floor = 1e-08
stat_epsilon = 1e-06


def factor_block(seeds, start, count, salt):
    columns = jnp.arange(count, dtype=jnp.int32) + start
    mixed = seeds[:, None] * 1103515245 + columns[None, :] * 40503 + salt * 7919
    mixed = jnp.bitwise_xor(mixed, jnp.right_shift(mixed, 15))
    mixed = mixed * 73244475
    mixed = jnp.bitwise_xor(mixed, jnp.right_shift(mixed, 13))
    level = jnp.bitwise_and(mixed, 255)
    return ((2 * level - 255).astype(jnp.float32) * (1.0 / 256.0)).astype(jnp.bfloat16)


def along_rows(rows, left):
    return jnp.sum(rows.astype(jnp.float32) * left.astype(jnp.float32), axis=1)


def gradient(scaled, left, right, members):
    weighted = (scaled[:, None] * right.astype(jnp.float32)).astype(jnp.bfloat16)
    total = lax.dot_general(
        left, weighted, (((0,), (0,)), ((), ())), preferred_element_type=jnp.float32
    )
    return total * (1.0 / (members * noise_scale))


def adam_step(weight, first, second, grad):
    first_new = beta_first * first + (1.0 - beta_first) * grad
    second_new = beta_second * second + (1.0 - beta_second) * grad * grad
    moved = weight.astype(jnp.float32) + learn_rate * first_new / (
        jnp.sqrt(second_new) + adam_floor
    )
    return (moved.astype(jnp.bfloat16), first_new, second_new)


def shards(
    tokens, seeds, fitness, gate_weight, up_weight, gate_first, up_first, gate_second, up_second
):
    members = seeds.shape[0]
    width_part = gate_weight.shape[0]
    unit_part = gate_weight.shape[1]
    width_start = lax.axis_index("fsdp") * width_part
    unit_start = lax.axis_index("pop") * unit_part
    left_gate = factor_block(seeds, width_start, width_part, 1)
    right_gate = factor_block(seeds, unit_start, unit_part, 2)
    left_up = factor_block(seeds, width_start, width_part, 3)
    right_up = factor_block(seeds, unit_start, unit_part, 4)
    gathered = lax.all_gather(tokens, "pop", axis=0, tiled=True)
    gate_along = along_rows(gathered, left_gate)
    up_along = along_rows(gathered, left_up)
    gate_right = right_gate.astype(jnp.float32)
    up_right = right_up.astype(jnp.float32)
    gate_term = (
        jnp.dot(gathered, gate_weight, preferred_element_type=jnp.float32)
        + noise_scale * gate_along[:, None] * gate_right
    )
    up_term = (
        jnp.dot(gathered, up_weight, preferred_element_type=jnp.float32)
        + noise_scale * up_along[:, None] * up_right
    )
    summed = lax.psum_scatter(
        jnp.concatenate([gate_term, up_term], axis=1), "fsdp", scatter_dimension=0, tiled=True
    )
    gate = summed[:, :unit_part]
    up = summed[:, unit_part:]
    hidden = (jax.nn.silu(gate) * up).astype(jnp.bfloat16)
    totals = lax.psum((jnp.sum(fitness), jnp.sum(fitness * fitness)), ("pop", "fsdp"))
    center = totals[0] / members
    spread = totals[1] / members - center * center
    scaled_local = (fitness - center) / jnp.sqrt(spread + stat_epsilon)
    scaled = lax.all_gather(scaled_local, ("pop", "fsdp"), axis=0, tiled=True)
    grad_gate = gradient(scaled, left_gate, right_gate, members)
    grad_up = gradient(scaled, left_up, right_up, members)
    gate_new, gate_first_new, gate_second_new = adam_step(
        gate_weight, gate_first, gate_second, grad_gate
    )
    up_new, up_first_new, up_second_new = adam_step(up_weight, up_first, up_second, grad_up)
    return (hidden, gate_new, up_new, gate_first_new, up_first_new, gate_second_new, up_second_new)


def solution(mesh):
    placed = (
        P("pop", "fsdp"),
        P(),
        P(("pop", "fsdp")),
        P("fsdp", "pop"),
        P("fsdp", "pop"),
        P("fsdp", "pop"),
        P("fsdp", "pop"),
        P("fsdp", "pop"),
        P("fsdp", "pop"),
    )
    return jax.shard_map(
        shards,
        mesh=mesh,
        in_specs=placed,
        out_specs=(
            P("fsdp", "pop"),
            P("fsdp", "pop"),
            P("fsdp", "pop"),
            P("fsdp", "pop"),
            P("fsdp", "pop"),
            P("fsdp", "pop"),
            P("fsdp", "pop"),
        ),
        check_vma=False,
    )
```

profile of v0, /device:TPU:0, one launch (start us, length us, event | category | flops | bytes accessed | tf_op | source)
XLA Modules:
  0.0 286.3 jit_solution(6194642691337779363)
XLA Ops:
  7.2 0.0 reduce-scatter.2.cloned.1.call-start
  7.2 0.7 broadcast_multiply_fusion.2
  7.9 9.5 %all_gather.6 = bf16[512,640]{1,0:T(8,128)(2,1)S(1)} all-gather(bf16[128,640]{1,0:T(8,128)(2,1)} %param.9), channel_id=1, replica_groups=mesh['pop'=4,'fsdp'=8] {'pop'}, dimensions={0}, use_global_device_ids=true | all-gather | bytes 819200 | tf_op jit(solution)/shard_map/all_gather | solution.py:57
  17.5 0.0 slice-start
  17.5 1.8 fusion.26
  19.2 0.0 slice-start.1
  19.3 7.0 %fusion.2 = f32[512,3584]{1,0:T(8,128)S(1)} fusion(bf16[512,640]{1,0:T(8,128)(2,1)S(1)} %all_gather.6, bf16[640,3584]{1,0:T(8,128)(2,1)} %param.13, f32[512]{0:T(512)S(1)} %get-tuple-element.19, s32[3584]{0:T(1024)S(1)} %add_multiply_fusion, s32[512]{0:T(512)S(1)} %broadcast_multiply_fusion.2), kind=kOutput, calls=%fused_computation.19 | convolution fusion | flops 2378170368 | bytes 12601344 | tf_op jit(solution)/shard_map/dot_general | solution.py:67
  26.2 0.0 slice-done
  26.2 0.0 slice-done.1
  26.3 4.7 %fusion = f32[512,3584]{1,0:T(8,128)S(1)} fusion(bf16[512,640]{1,0:T(8,128)(2,1)S(1)} %all_gather.6, bf16[640,3584]{1,0:T(8,128)(2,1)S(1)} %bitcast.5, s32[3584]{0:T(1024)S(1)} %add_multiply_fusion, s32[512]{0:T(512)S(1)} %broadcast_multiply_fusion.2, f32[512]{0:T(512)S(1)} %get-tuple-element.20), kind=kOutput, calls=%fused_computation.17 | convolution fusion | flops 2378170368 | bytes 12601344 | tf_op jit(solution)/shard_map/dot_general | solution.py:63
  30.9 5.5 %pad_maximum_fusion = f32[512,7168]{1,0:T(8,128)} fusion(f32[512,3584]{1,0:T(8,128)S(1)} %fusion.2, f32[512,3584]{1,0:T(8,128)S(1)} %fusion), kind=kLoop, calls=%fused_computation | loop fusion | flops 3670016 | bytes 29360128 | tf_op jit(solution)/shard_map/concatenate | solution.py:71
  36.4 0.0 copy-start
  36.4 0.0 reduce-scatter.2.cloned.1.call-update
  36.5 0.6 copy-done
  37.1 0.6 fusion.63
  37.7 46.0 %all-reduce.1 = (f32[]{:T(128)}, f32[]{:T(128)}) all-reduce(f32[]{:T(128)} %get-tuple-element.10, f32[]{:T(128)} %get-tuple-element.9), channel_id=1, replica_groups=mesh['pop'=4,'fsdp'=8] {'pop','fsdp'}, use_global_device_ids=true, to_apply=%region_6.7 | all-reduce | flops 2 | bytes 16 | tf_op jit(solution)/shard_map/psum | solution.py:76
  86.3 0.1 divide_dynamic-update-slice_fusion
  86.4 44.0 %all-reduce = f32[512]{0:T(512)S(1)} all-reduce(f32[512]{0:T(512)S(1)} %divide_dynamic-update-slice_fusion), channel_id=1, replica_groups=mesh['pop'=4,'fsdp'=8] {'pop','fsdp'}, use_global_device_ids=true, to_apply=%add | all-reduce | flops 512 | bytes 4096
  130.4 20.1 %add_convert_fusion.1 = (bf16[640,3584]{1,0:T(8,128)(2,1)}, f32[640,3584]{1,0:T(8,128)}, f32[640,3584]{1,0:T(8,128)}) fusion(bf16[640,3584]{1,0:T(8,128)(2,1)} %param.12, f32[640,3584]{1,0:T(8,128)} %param.14, f32[640,3584]{1,0:T(8,128)} %param.16, f32[512]{0:T(512)S(1)} %all-reduce, s32[3584]{0:T(1024)S(1)} %add_multiply_fusion, ...), kind=kOutput, calls=%fused_computation.10 | convolution fusion | flops 2414542848 | bytes 45896192 | tf_op jit(solution)/shard_map/dot_general | solution.py:30
  150.6 20.3 %add_convert_fusion = (bf16[640,3584]{1,0:T(8,128)(2,1)}, f32[640,3584]{1,0:T(8,128)}, f32[640,3584]{1,0:T(8,128)}) fusion(bf16[640,3584]{1,0:T(8,128)(2,1)} %param.13, f32[640,3584]{1,0:T(8,128)} %param.15, f32[640,3584]{1,0:T(8,128)} %param.17, f32[512]{0:T(512)S(1)} %all-reduce, s32[3584]{0:T(1024)S(1)} %add_multiply_fusion, ...), kind=kOutput, calls=%fused_computation.7 | convolution fusion | flops 2414542848 | bytes 45896192 | tf_op jit(solution)/shard_map/dot_general | solution.py:30
  170.8 106.2 %reduce-scatter.2.cloned.1.call-done = f32[64,7168]{1,0:T(8,128)} async-done(((f32[512,7168]{1,0:T(8,128)}), f32[64,7168]{1,0:T(8,128)}) %reduce-scatter.2.cloned.1.call-update) | async-done | bytes 1835024 | tf_op jit(solution)/shard_map/reduce_scatter | solution.py:70
  277.0 2.5 fusion.42
  (5 shorter events, 0.0 us)
Async XLA Ops:
  7.2 269.8 %reduce-scatter.2.cloned.1.call-start = ((), (), s32[]{:S(2)}) async-start(), calls=%async_computation.1 | async-start | bytes 16515072 | tf_op jit(solution)/shard_map/reduce_scatter | solution.py:70
  17.5 8.8 %slice-start = ((s8[4587520]{0:T(1024)(128)(4,1)}), s8[4194304]{0:T(1024)(128)(4,1)S(1)}, s32[]{:S(2)}) async-start(s8[4587520]{0:T(1024)(128)(4,1)} %bitcast.4), calls=%async_computation.2 | async-start | bytes 8388608
  19.2 7.0 %slice-start.1 = ((s8[4587520]{0:T(1024)(128)(4,1)}), s8[393216]{0:T(1024)(128)(4,1)S(1)}, s32[]{:S(2)}) async-start(s8[4587520]{0:T(1024)(128)(4,1)} %bitcast.4), calls=%async_computation.3 | async-start | bytes 786432
  36.4 0.7 copy-start
Sparse Core Ops, SparseCore 0:
  36.6 240.3 reduce-scatter.1
where the time goes:
time: 287 us; the launch traced here: 286 us
  waiting for transfers between devices  106 us (37%)
  blocking collectives  99.5 us (35%)
  matrix products  52 us (18%)
  between operations  16.7 us (6%)
  other arithmetic  11.1 us (4%)
    reduce_scatter x1, waiting for transfers between devices, shards(): lax.psum_scatter(jnp.concatenate([gate_term, up_term], axis=1), 'fsdp', s...  106 us
    psum x1, blocking collectives, shards(): lax.psum((jnp.sum(fitness), jnp.sum(fitness * fitness)), ('pop', 'fsdp'))  46 us
    unnamed x1, blocking collectives  44 us
    dot_general x2, matrix products, gradient(): lax.dot_general(left, weighted, (((0,), (0,)), ((), ())), preferred_eleme...  40.4 us
    all_gather x1, blocking collectives, shards(): gathered = lax.all_gather(tokens, 'pop', axis=0, tiled=True)  9.54 us
    dot_general x1, matrix products, shards(): jnp.dot(gathered, up_weight, preferred_element_type=jnp.float32)  6.98 us
  transfers between devices with their start and end apart: 1, of which 1 were waited for; matrix products, arithmetic and copies ran while one was open for 14% of the time, Pallas kernels for 0%

commit v1 on v0

v1 whole, which is shorter than its diff:
```python
import functools

import jax
import jax.numpy as jnp
from jax import lax
from jax.experimental import pallas as pl
from jax.experimental.pallas import tpu as pltpu
from jax.sharding import PartitionSpec as P

noise_scale = 0.01
learn_rate = 0.002
beta_first = 0.9
beta_second = 0.99
adam_floor = 1e-08
stat_epsilon = 1e-06

f32 = jnp.float32
bf16 = jnp.bfloat16
wire = jnp.float16


def mixed_levels(mixed):
    mixed = jnp.bitwise_xor(mixed, jnp.right_shift(mixed, 15))
    mixed = mixed * 73244475
    mixed = jnp.bitwise_xor(mixed, jnp.right_shift(mixed, 13))
    level = jnp.bitwise_and(mixed, 255)
    return (2 * level - 255).astype(f32) * (1.0 / 256.0)


def member_part(seeds):
    return seeds * 1103515245


def column_part(columns, salt):
    return columns * 40503 + salt * 7919


def factor_levels(seed, column, salt):
    return mixed_levels(member_part(seed) + column_part(column, salt))


def factor_block(seeds, start, count, salt):
    columns = jnp.arange(count, dtype=jnp.int32) + start
    return factor_levels(seeds[:, None], columns[None, :], salt)


def factor_block_turned(seeds, start, count, salt):
    columns = jnp.arange(count, dtype=jnp.int32) + start
    return factor_levels(seeds[None, :], columns[:, None], salt).astype(bf16)


def adam_kernel(scale, row_tile, extra, *refs):
    left, member, unit, scaled, kept_tokens, weight, first, second = refs[:8]
    weight_new, first_new, second_new, kept = refs[8 + extra :]
    weighted = (scaled[...] * mixed_levels(member[...] + unit[...])).astype(bf16)
    kept[...] = jnp.dot(kept_tokens[...], weight[...], preferred_element_type=f32)
    for start in range(0, left.shape[0], row_tile):
        rows = slice(start, start + row_tile)
        g = jnp.dot(left[rows, :], weighted, preferred_element_type=f32) * scale
        f = beta_first * first[rows, :] + (1.0 - beta_first) * g
        s = beta_second * second[rows, :] + (1.0 - beta_second) * g * g
        first_new[rows, :] = f
        second_new[rows, :] = s
        moved = weight[rows, :].astype(f32) + learn_rate * f / (jnp.sqrt(s) + adam_floor)
        weight_new[rows, :] = moved.astype(bf16)


def adam_part(left, member, unit, scaled, kept_tokens, weight, first, second, before, start, tile, steps):
    width, units = weight.shape
    members = member.shape[0]
    row_tile = 128 if width % 128 == 0 else width
    kept_rows = kept_tokens.shape[0]
    base = start // tile
    full = lambda dtype: jax.ShapeDtypeStruct((width, units), dtype)
    big = lambda: pl.BlockSpec((width, tile), lambda j: (0, base + j))
    in_specs = [
        pl.BlockSpec((width, members), lambda j: (0, 0)),
        pl.BlockSpec((members, 1), lambda j: (0, 0)),
        pl.BlockSpec((1, tile), lambda j: (0, base + j)),
        pl.BlockSpec((members, 1), lambda j: (0, 0)),
        pl.BlockSpec((kept_rows, width), lambda j: (0, 0)),
        big(),
        big(),
        big(),
    ]
    args = [left, member, unit, scaled, kept_tokens, weight, first, second]
    aliases = {}
    if before is not None:
        args += list(before)
        aliases = {8: 0, 9: 1, 10: 2}
    extra = len(args) - 8
    in_specs += [pl.BlockSpec(memory_space=pl.ANY)] * extra
    return pl.pallas_call(
        functools.partial(adam_kernel, 1.0 / (members * noise_scale), row_tile, extra),
        grid=(steps,),
        in_specs=in_specs,
        out_specs=[big(), big(), big(), pl.BlockSpec((kept_rows, tile), lambda j: (0, j))],
        out_shape=[
            full(bf16),
            full(f32),
            full(f32),
            jax.ShapeDtypeStruct((kept_rows, tile * steps), f32),
        ],
        input_output_aliases=aliases,
        compiler_params=pltpu.CompilerParams(vmem_limit_bytes=50 * 1024 * 1024),
        cost_estimate=pl.CostEstimate(
            flops=2 * width * tile * steps * (members + kept_rows),
            bytes_accessed=20 * width * tile * steps,
            transcendentals=0,
        ),
    )(*args)


def sort_kernel(orders, share, index, seeds, columns, *refs):
    kinds = len(orders)
    pieces = refs[: -3 * kinds - 1]
    turned, alongs, ids = (refs[len(pieces) + i * kinds :][:kinds] for i in range(3))
    held = refs[-1]
    per_piece = pieces[0].shape[0] // share
    for p, piece in enumerate(pieces):
        for k in range(per_piece):
            held[p * per_piece + k] = piece[k * share : (k + 1) * share, :]
    for mask in range(held.shape[0]):
        rows = held[index[0, mask]]
        block = pl.multiple_of(index[1, mask] * share, share)
        member = member_part(seeds[pl.ds(block, share), :])
        wide = rows.astype(f32)
        along = [
            noise_scale
            * jnp.sum(wide * mixed_levels(member + columns[i : i + 1, :]), axis=1, keepdims=True)
            for i in range(2)
        ]
        for kind, order in enumerate(orders):
            at = order.index(mask) * share
            turned[kind][at : at + share, :] = rows
            ids[kind][at : at + share, :] = member
            for i in range(2):
                alongs[kind][at : at + share, i : i + 1] = along[i]


def sort_blocks(pieces, index, seeds, columns, orders):
    members = seeds.shape[0]
    width = pieces[0].shape[1]
    shares = len(orders[0])
    share = members // shares
    kinds = len(orders)
    whole = pl.BlockSpec(memory_space=pltpu.VMEM)
    outs = pl.pallas_call(
        functools.partial(sort_kernel, orders, share),
        in_specs=[pl.BlockSpec(memory_space=pltpu.SMEM)] + [whole] * (2 + len(pieces)),
        out_specs=[whole] * (3 * kinds),
        out_shape=[jax.ShapeDtypeStruct((members, width), bf16)] * kinds
        + [jax.ShapeDtypeStruct((members, 2), f32)] * kinds
        + [jax.ShapeDtypeStruct((members, 1), jnp.int32)] * kinds,
        scratch_shapes=[pltpu.VMEM((shares, share, width), bf16)],
        compiler_params=pltpu.CompilerParams(vmem_limit_bytes=32 * 1024 * 1024),
    )(index, seeds[:, None], columns, *pieces)
    return outs[:kinds], outs[kinds : 2 * kinds], outs[2 * kinds :]


def block_order(bits):
    order = [0]
    for bit in reversed(bits):
        order = order + [mask ^ (1 << bit) for mask in order]
    return order


def shards(
    tokens, seeds, fitness, gate_weight, up_weight, gate_first, up_first, gate_second, up_second
):
    members = seeds.shape[0]
    width_part, unit_part = gate_weight.shape
    shares = lax.axis_size("fsdp")
    share = members // shares
    me = lax.axis_index("fsdp")
    width_start = me * width_part
    unit_start = lax.axis_index("pop") * unit_part
    levels = shares.bit_length() - 1
    across = list(range(levels))
    along_first = [1, 0] + across[2:] if levels > 1 else across

    def exchange(x, bit, axis="fsdp"):
        size = lax.axis_size(axis)
        return lax.ppermute(x, axis, [(i, i ^ (1 << bit)) for i in range(size)])

    def after(x, *others):
        return lax.optimization_barrier((x, others))[0]

    pops = lax.axis_size("pop")
    pop = lax.axis_index("pop")
    per_pop = shares // pops
    pieces = [tokens]
    for mask in reversed(range(1, pops)):
        pieces.insert(1, lax.ppermute(tokens, "pop", [(i, i ^ mask) for i in range(pops)]))

    fit = lax.dynamic_update_slice(
        jnp.zeros((members,), f32), fitness, ((pop * shares + me) * fitness.shape[0],)
    )
    turned_gate = factor_block_turned(seeds, width_start, width_part, 1)
    for bit in range(levels):
        fit = fit + exchange(fit, bit)
        if bit == 0:
            turned_up = factor_block_turned(after(seeds, fit), width_start, width_part, 3)

    masks = jnp.arange(shares)
    blocks = jnp.bitwise_xor(me, masks)
    slots = jnp.bitwise_xor(blocks // per_pop, pop) * per_pop + blocks % per_pop
    features = jnp.arange(width_part, dtype=jnp.int32) + width_start
    orders = [block_order(across), block_order(along_first)]
    bits_of = [across, along_first]
    tokens_of, along_of, member_of = sort_blocks(
        pieces,
        jnp.stack([slots, blocks]).astype(jnp.int32),
        seeds,
        jnp.stack([column_part(features, 1), column_part(features, 3)]),
        orders,
    )

    fit = after(fit, *tokens_of)
    for bit in range(pops.bit_length() - 1):
        fit = fit + exchange(fit, bit, "pop")
    all_fitness = fit

    columns = jnp.arange(unit_part, dtype=jnp.int32) + unit_start
    member = member_part(seeds)[:, None]

    center = jnp.mean(all_fitness)
    spread = jnp.mean(jnp.square(all_fitness - center))
    scaled = ((all_fitness - center) / jnp.sqrt(spread + stat_epsilon))[:, None]

    parts = 2
    tile = unit_part // parts
    per_call = 2 if tile % 256 == 0 else 1
    half = members // 2
    plan = [(0, "gate", 1), (0, "up", 0), (1, "gate", 0), (1, "up", 0)]
    state = {
        "gate": (turned_gate, column_part(columns, 2)[None, :], gate_weight, gate_first, gate_second),
        "up": (turned_up, column_part(columns, 4)[None, :], up_weight, up_first, up_second),
    }

    def term(name, kind, at, rows):
        along = along_of[kind][rows, {"gate": 0, "up": 1}[name]][:, None]
        unit = state[name][1][:, at * tile : (at + 1) * tile]
        return along * mixed_levels(member_of[kind][rows] + unit)

    sent = []
    for at, name, kind in plan:
        weight = state[name][2][:, at * tile : (at + 1) * tile]
        rows = tokens_of[kind][half:]
        if sent:
            rows = after(rows, partial)
        partial = jnp.dot(rows, weight, preferred_element_type=f32)
        partial = (partial + term(name, kind, at, slice(half, None))).astype(wire)
        sent.append(exchange(partial, bits_of[kind][0]))

    updated = {"gate": None, "up": None}
    kept_of = {}

    summed = {}
    running = {}

    def update(index, before=(), held=()):
        at, name, kind = plan[index]
        left, unit, weight, first, second = state[name]
        tied, _ = lax.optimization_barrier((scaled, list(before)))
        *done, kept = adam_part(
            left,
            member,
            unit,
            tied,
            tokens_of[kind][:half],
            weight,
            first,
            second,
            updated[name],
            at * tile,
            tile // per_call,
            per_call,
        )
        updated[name] = done
        kept_of[at, name] = kept
        for other in held:
            running[other] = after(running[other], kept)


    def reduce_step(index, level):
        at, name, kind = plan[index]
        if level == 0:
            kept = kept_of[at, name]
            running[index] = [kept, after(sent[index], kept)]
        *summands, arrived = running[index]
        rows = arrived.shape[0] // 2

        def added(part):
            total = summands[0][part]
            if level == 0:
                total = total + term(name, kind, at, part)
            for x in summands[1:] + [arrived]:
                total = total + x[part].astype(f32)
            return total

        if level == levels - 1:
            summed[name, at] = added(slice(None))
            return None
        outgoing = added(slice(rows, 2 * rows)).astype(wire)
        running[index] = [added(slice(0, rows)), exchange(outgoing, bits_of[kind][level + 1])]
        return outgoing

    update(0)
    update(1)
    out_0 = reduce_step(0, 0)
    out_1 = reduce_step(1, 0)
    update(2, [out_0, out_1])
    out_2 = reduce_step(2, 0)
    out_3 = reduce_step(1, 1)
    update(3, [out_2, out_3], [0, 2])
    out_4 = reduce_step(3, 0)
    for index in (0, 2):
        running[index] = after(running[index], out_4)
    reduce_step(0, 1)
    reduce_step(2, 1)
    reduce_step(3, 1)
    for index in range(len(plan)):
        for level in range(2, levels):
            reduce_step(index, level)

    def finished(name):
        return jnp.concatenate([summed[name, at] for at in range(parts)], axis=1)

    hidden = (jax.nn.silu(finished("gate")) * finished("up")).astype(bf16)
    gate_new, gate_first_new, gate_second_new = updated["gate"]
    up_new, up_first_new, up_second_new = updated["up"]
    return (hidden, gate_new, up_new, gate_first_new, up_first_new, gate_second_new, up_second_new)


def solution(mesh):
    placed = (P("pop", "fsdp"), P(), P(("pop", "fsdp"))) + (P("fsdp", "pop"),) * 6
    return jax.shard_map(
        shards,
        mesh=mesh,
        in_specs=placed,
        out_specs=(P("fsdp", "pop"),) * 7,
        check_vma=False,
    )
```

time: 287 us -> 146 us (0.51)
  blocking collectives: 99.5 us -> 0 us
  waiting for transfers between devices: 106 us -> 32.9 us
  Pallas kernels: 0 us -> 46.7 us
  matrix products: 52 us -> 10.1 us
  starting transfers between devices: 0.04 us -> 26.1 us
  between operations: 16.7 us -> 2.39 us
  other arithmetic: 11.1 us -> 24.1 us
  local copies, waits for them, and re-layouts: 0.64 us -> 3.84 us
    reduce_scatter x1 -> x0, waiting for transfers between devices: 106 us -> none  [shards(): lax.psum_scatter(jnp.concatenate([gate_term, up_term], axis=1), 'fsdp', s...]
    pallas_call x0 -> x5, Pallas kernels: none -> 46.7 us  [the longest x4 44.5 us: adam_part(): pl.pallas_call(functools.partial(adam_kernel, 1.0 / (members * noise_scal...]
    psum x1 -> x0, blocking collectives: 46 us -> none  [shards(): lax.psum((jnp.sum(fitness), jnp.sum(fitness * fitness)), ('pop', 'fsdp'))]
    unnamed x1 -> x0, blocking collectives: 44 us -> none
    dot_general x4, matrix products: 52 us -> 10.1 us  [shards(): partial = jnp.dot(rows, weight, preferred_element_type=f32)]
    ppermute x0 -> x20, waiting for transfers between devices: none -> 32.9 us  [the longest x17 32.9 us: exchange(): return lax.ppermute(x, axis, [(i, i ^ 1 << bit) for i in range(size)])]
    ppermute x0 -> x20, starting transfers between devices: none -> 26.1 us  [the longest x17 22.8 us: exchange(): return lax.ppermute(x, axis, [(i, i ^ 1 << bit) for i in range(size)])]
    add x0 -> x16, other arithmetic: none -> 13.3 us  [the longest x7 12.4 us: added(): total = total + x[part].astype(f32)]
  transfers between devices with their start and end apart: 1 -> 20, of which waited for: 1 -> 6; matrix products, arithmetic and copies ran while one was open for 14% -> 24% of each run, Pallas kernels for 0% -> 30%
where the time goes in v1:
time: 146 us
  Pallas kernels  46.7 us (32%)
  waiting for transfers between devices  32.9 us (23%)
  starting transfers between devices  26.1 us (18%)
  other arithmetic  24.1 us (17%)
  matrix products  10.1 us (7%)
  local copies, waits for them, and re-layouts  3.84 us (3%)
  between operations  2.39 us (2%)
    pallas_call x4, Pallas kernels, adam_part(): pl.pallas_call(functools.partial(adam_kernel, 1.0 / (members * noise_scal...  44.5 us
    ppermute x17, waiting for transfers between devices, exchange(): return lax.ppermute(x, axis, [(i, i ^ 1 << bit) for i in range(size)])  32.9 us
    ppermute x17, starting transfers between devices, exchange(): return lax.ppermute(x, axis, [(i, i ^ 1 << bit) for i in range(size)])  22.8 us
    add x7, other arithmetic, added(): total = total + x[part].astype(f32)  12.4 us
    dot_general x4, matrix products, shards(): partial = jnp.dot(rows, weight, preferred_element_type=f32)  10.1 us
    convert_element_type x5, other arithmetic, reduce_step(): outgoing = added(slice(rows, 2 * rows)).astype(wire)  5.4 us
    ppermute x3, starting transfers between devices, shards(): lax.ppermute(tokens, 'pop', [(i, i ^ mask) for i in range(pops)])  3.21 us
  transfers between devices with their start and end apart: 20, of which 6 were waited for; matrix products, arithmetic and copies ran while one was open for 24% of the time, Pallas kernels for 30%

profile of v1, /device:TPU:0, one launch (start us, length us, event | category | flops | bytes accessed | tf_op | source)
XLA Modules:
  0.0 146.0 jit_solution(4501554988467385585)
XLA Ops:
  0.6 3.0 %collective-permute-start.4 = (bf16[128,640]{1,0:T(8,128)(2,1)}, bf16[128,640]{1,0:T(8,128)(2,1)S(1)}, u32[]{:S(2)}, u32[]{:S(2)}) collective-permute-start(bf16[128,640]{1,0:T(8,128)(2,1)} %refs_0_.1), channel_id=1, source_target_pairs={{0,16},{8,24},{16,0},{24,8},{1,17},{9,25},{17,1},{25,9},{2,18},{10... | collective-permute-start | bytes 491528 | tf_op jit(solution)/shard_map/ppermute | solution.py:194
  3.6 0.2 collective-permute-start.5
  3.9 0.8 dynamic_update_slice.5
  4.7 2.0 %collective-permute-start = (f32[512]{0:T(512)S(1)}, f32[512]{0:T(512)S(1)}, u32[]{:S(2)}, u32[]{:S(2)}) collective-permute-start(f32[512]{0:T(512)S(1)} %dynamic_update_slice.5), channel_id=1, source_target_pairs={{0,1},{1,0},{2,3},{3,2},{4,5},{5,4},{6,7},{7,6},{8,9},{9,8},{10,11... | collective-permute-start | bytes 6152 | tf_op jit(solution)/shard_map/ppermute | solution.py:184
  6.7 0.7 broadcast_multiply_fusion.1
  7.6 0.6 fusion.38.refs_0_
  8.1 0.1 copy.23.refs_1_
  8.3 0.8 copy.22.seeds
  9.1 0.8 add_dynamic-update-slice_fusion
  10.0 1.6 %collective-permute-start.1 = (f32[512]{0:T(512)S(1)}, f32[512]{0:T(512)S(1)}, u32[]{:S(2)}, u32[]{:S(2)}) collective-permute-start(f32[512]{0:T(512)S(1)} %add_dynamic-update-slice_fusion), channel_id=1, source_target_pairs={{0,2},{1,3},{2,0},{3,1},{4,6},{5,7},{6,4},{7,5},{8,10},{9,11},{10,... | collective-permute-start | bytes 6152 | tf_op jit(solution)/shard_map/ppermute | solution.py:184
  11.5 0.7 broadcast_multiply_fusion
  12.2 1.3 collective-permute-done.1
  13.5 2.6 %collective-permute-start.2 = (f32[512]{0:T(512)S(1)}, f32[512]{0:T(512)S(1)}, u32[]{:S(2)}, u32[]{:S(2)}) collective-permute-start(f32[512]{0:T(512)S(1)} %add.489), channel_id=1, source_target_pairs={{0,4},{1,5},{2,6},{3,7},{4,0},{5,1},{6,2},{7,3},{8,12},{9,13},{10,... | collective-permute-start | bytes 6152 | tf_op jit(solution)/shard_map/ppermute | solution.py:184
  16.1 0.6 fusion.45.refs_0_
  16.7 1.3 collective-permute-done.2
  18.1 2.2 %shard_map.144 = (bf16[512,640]{1,0:T(8,128)(2,1)S(1)}, bf16[512,640]{1,0:T(8,128)(2,1)S(1)}, f32[512,2]{1,0:T(8,128)S(1)}, f32[512,2]{1,0:T(8,128)S(1)}, s32[512,1]{1,0:T(8,128)S(1)}, /*index=5*/s32[512,1]{1,0:T(8,128)S(1)}) custom-call(s32[2,8]{1,0:T(2,128)S(1)} %pad_add_fusion.1.index, s32[512,1]{1,0:T(8,128)S(1)} %copy.22.seeds, ...), custom_call_target="tpu_custom_call" | custom-call | tf_op jit(solution)/shard_map/pallas_call | solution.py:148
  20.2 0.1 slice_reduce_fusion
  20.4 0.1 slice_reduce_fusion.2
  20.5 0.1 multiply_reduce_fusion.2
  20.6 0.1 multiply_reduce_fusion.8
  20.7 0.2 multiply_reduce_fusion.3
  21.0 0.2 multiply_reduce_fusion
  21.2 0.1 slice_reduce_fusion.1
  21.5 3.9 %fusion = f16[256,1792]{1,0:T(8,128)(2,1)} fusion(bf16[640,3584]{1,0:T(8,128)(2,1)} %refs_5_.6, f32[256]{0:T(256)S(1)} %multiply_reduce_fusion.2, s32[1792]{0:T(1024)S(1)} %get-tuple-element.104, s32[256]{0:T(256)S(1)} %slice_reduce_fusion.1, bf16[512,640]{1,0:T(8,128)(2,1)S(1)} %get-tuple-element.49), kind=kOutput, calls=%fused_computation.12 | convolution fusion | flops 593166336 | bytes 3549184 | tf_op jit(solution)/shard_map/dot_general | solution.py:252
  25.3 2.1 %fusion.1 = f16[256,1792]{1,0:T(8,128)(2,1)} fusion(bf16[256,640]{1,0:T(8,128)(2,1)S(1)} %get-tuple-element.75, bf16[640,3584]{1,0:T(8,128)(2,1)S(1)} %copy-done.1, f32[256]{0:T(256)S(1)} %get-tuple-element.100, s32[1792]{0:T(1024)S(1)} %get-tuple-element.102, s32[256]{0:T(256)S(1)} %slice_reduce_fusion), kind=kOutput, calls=%fused_computation.13 | convolution fusion | flops 593166336 | bytes 3549184 | tf_op jit(solution)/shard_map/dot_general | solution.py:252
  27.4 2.0 %fusion.2 = f16[256,1792]{1,0:T(8,128)(2,1)} fusion(bf16[256,640]{1,0:T(8,128)(2,1)S(1)} %get-tuple-element.75, bf16[640,3584]{1,0:T(8,128)(2,1)S(1)} %bitcast.7, f32[256]{0:T(256)S(1)} %get-tuple-element.99, s32[1792]{0:T(1024)S(1)} %get-tuple-element.103, s32[256]{0:T(256)S(1)} %slice_reduce_fusion), kind=kOutput, calls=%fused_computation.14 | convolution fusion | flops 593166336 | bytes 3549184 | tf_op jit(solution)/shard_map/dot_general | solution.py:252
  29.6 1.2 collective-permute-start.11
  30.8 0.9 collective-permute-start.10
  31.7 1.6 %collective-permute-start.8 = (f16[256,1792]{1,0:T(8,128)(2,1)}, f16[256,1792]{1,0:T(8,128)(2,1)S(1)}, u32[]{:S(2)}, u32[]{:S(2)}) collective-permute-start(f16[256,1792]{1,0:T(8,128)(2,1)} %fusion), channel_id=1, source_target_pairs={{0,2},{1,3},{2,0},{3,1},{4,6},{5,7},{6,4},{7,5},{8,10},{9,11},{10,... | collective-permute-start | bytes 2752520 | tf_op jit(solution)/shard_map/ppermute | solution.py:184
  33.3 1.5 %collective-permute-start.7 = (f32[512]{0:T(512)S(1)}, f32[512]{0:T(512)S(1)}, u32[]{:S(2)}, u32[]{:S(2)}) collective-permute-start(f32[512]{0:T(512)S(1)} %add.499), channel_id=1, source_target_pairs={{0,16},{8,24},{16,0},{24,8},{1,17},{9,25},{17,1},{25,9},{2,18},{10... | collective-permute-start | bytes 6152 | tf_op jit(solution)/shard_map/ppermute | solution.py:184
  34.8 2.1 %fusion.3 = f16[256,1792]{1,0:T(8,128)(2,1)} fusion(bf16[256,640]{1,0:T(8,128)(2,1)S(1)} %get-tuple-element.75, bf16[640,3584]{1,0:T(8,128)(2,1)S(1)} %copy-done.1, s32[1792]{0:T(1024)S(1)} %get-tuple-element.101, f32[256]{0:T(256)S(1)} %get-tuple-element.100, s32[256]{0:T(256)S(1)} %slice_reduce_fusion), kind=kOutput, calls=%fused_computation.15 | convolution fusion | flops 593166336 | bytes 3549184 | tf_op jit(solution)/shard_map/dot_general | solution.py:252
  36.8 1.1 collective-permute-start.13
  38.0 0.6 fusion.127
  39.2 0.6 multiply_reduce_fusion.9
  40.5 0.1 copy.24.refs_3_
  40.7 11.3 %shard_map.145 = (bf16[640,3584]{1,0:T(8,128)(2,1)}, f32[640,3584]{1,0:T(8,128)}, f32[640,3584]{1,0:T(8,128)}, f32[256,1792]{1,0:T(8,128)S(1)}) custom-call(bf16[640,512]{1,0:T(8,128)(2,1)S(1)} %fusion.38.refs_0_, s32[512,1]{1,0:T(8,128)S(1)} %copy.23.refs_1_, s32[1,3584]{1,0:T(1,128)S(1)} %get-tuple-element.122.refs_2_, f32[512,1]{1,0:T(8,128)S(1)} %copy.24.refs_3_, ...), custom_call_target="tpu_custom_call" | custom-call | flops 1761607680 | bytes 22937600 | tf_op jit(solution)/shard_map/pallas_call | solution.py:93
  51.9 11.1 %shard_map.146 = (bf16[640,3584]{1,0:T(8,128)(2,1)}, f32[640,3584]{1,0:T(8,128)}, f32[640,3584]{1,0:T(8,128)}, f32[256,1792]{1,0:T(8,128)S(1)}) custom-call(bf16[640,512]{1,0:T(8,128)(2,1)S(1)} %fusion.45.refs_0_, s32[512,1]{1,0:T(8,128)S(1)} %copy.23.refs_1_, s32[1,3584]{1,0:T(1,128)S(1)} %get-tuple-element.121.refs_2_, f32[512,1]{1,0:T(8,128)S(1)} %copy.24.refs_3_, ...), custom_call_target="tpu_custom_call" | custom-call | flops 1761607680 | bytes 22937600 | tf_op jit(solution)/shard_map/pallas_call | solution.py:93
  63.0 0.9 copy-done.5
  64.0 2.8 %fusion.53 = (f32[128,1792]{1,0:T(8,128)S(1)}, f16[128,1792]{1,0:T(8,128)(2,1)}) fusion(f32[256,1792]{1,0:T(8,128)S(1)} %get-tuple-element.51, f16[256,1792]{1,0:T(8,128)(2,1)} %copy-done.5, f32[128]{0:T(128)S(1)} %get-tuple-element.91, s32[1792]{0:T(1024)S(1)} %get-tuple-element.104, s32[128]{0:T(128)S(1)} %get-tuple-element.89, ...), kind=kLoop, calls=%fused_computation.85 | loop fusion | flops 6651904 | bytes 4137984 | tf_op jit(solution)/shard_map/add | solution.py:299
  66.7 0.9 collective-permute-start.9
  67.6 5.2 %collective-permute-done.10 = f16[256,1792]{1,0:T(8,128)(2,1)} collective-permute-done((f16[256,1792]{1,0:T(8,128)(2,1)}, f16[256,1792]{1,0:T(8,128)(2,1)}, u32[]{:S(2)}, u32[]{:S(2)}) %collective-permute-start.10) | collective-permute-done | bytes 917536 | tf_op jit(solution)/shard_map/ppermute | solution.py:184
  72.8 3.2 %fusion.88 = (f32[128,1792]{1,0:T(8,128)}, f16[128,1792]{1,0:T(8,128)(2,1)}) fusion(f32[256,1792]{1,0:T(8,128)S(1)} %get-tuple-element.56, f16[256,1792]{1,0:T(8,128)(2,1)} %collective-permute-done.10, f32[128]{0:T(128)S(1)} %get-tuple-element.94, s32[128]{0:T(128)S(1)} %get-tuple-element.97, s32[1792]{0:T(1024)S(1)} %get-tuple-element.102, ...), kind=kLoop, calls=%fused_computation.120 | loop fusion | flops 6651904 | bytes 4137984 | tf_op jit(solution)/shard_map/add | solution.py:299
  76.0 1.6 %collective-permute-start.12 = (f16[128,1792]{1,0:T(8,128)(2,1)}, f16[128,1792]{1,0:T(8,128)(2,1)}, u32[]{:S(2)}, u32[]{:S(2)}) collective-permute-start(f16[128,1792]{1,0:T(8,128)(2,1)} %get-tuple-element.114), channel_id=1, source_target_pairs={{0,2},{1,3},{2,0},{3,1},{4,6},{5,7},{6,4},{7,5},{8,10},{9,11},{10,... | collective-permute-start | bytes 1376264 | tf_op jit(solution)/shard_map/ppermute | solution.py:184
  77.6 0.1 copy.28.refs_3_
  77.7 11.1 %shard_map.147 = (bf16[640,3584]{1,0:T(8,128)(2,1)}, f32[640,3584]{1,0:T(8,128)}, f32[640,3584]{1,0:T(8,128)}, f32[256,1792]{1,0:T(8,128)S(1)}) custom-call(bf16[640,512]{1,0:T(8,128)(2,1)S(1)} %fusion.38.refs_0_, s32[512,1]{1,0:T(8,128)S(1)} %copy.23.refs_1_, ...), custom_call_target="tpu_custom_call", output_to_operand_aliasing={{0}: (8, {}), {1}: (9, {}), {2}: (10, {})} | custom-call | flops 1761607680 | bytes 22937600 | tf_op jit(solution)/shard_map/pallas_call | solution.py:93
  88.8 3.3 %fusion.105 = (f32[128,1792]{1,0:T(8,128)}, f16[128,1792]{1,0:T(8,128)(2,1)S(1)}) fusion(f32[256,1792]{1,0:T(8,128)S(1)} %get-tuple-element.65, f16[256,1792]{1,0:T(8,128)(2,1)} %collective-permute-done.11, f32[128]{0:T(128)S(1)} %get-tuple-element.93, s32[128]{0:T(128)S(1)} %get-tuple-element.97, s32[1792]{0:T(1024)S(1)} %get-tuple-element.103, ...), kind=kLoop, calls=%fused_computation.137 | loop fusion | flops 6651904 | bytes 4137984 | tf_op jit(solution)/shard_map/add | solution.py:299
  92.1 0.4 collective-permute-start.15
  92.5 1.0 fusion.118
  93.5 2.7 %collective-permute-start.17 = (f16[64,1792]{1,0:T(8,128)(2,1)S(1)}, f16[64,1792]{1,0:T(8,128)(2,1)S(1)}, u32[]{:S(2)}, u32[]{:S(2)}) collective-permute-start(f16[64,1792]{1,0:T(8,128)(2,1)S(1)} %fusion.118), channel_id=1, source_target_pairs={{0,4},{1,5},{2,6},{3,7},{4,0},{5,1},{6,2},{7,3},{8,12},{9,13},{10,... | collective-permute-start | bytes 688136 | tf_op jit(solution)/shard_map/ppermute | solution.py:184
  96.2 0.1 copy.30.refs_3_
  96.4 11.1 %shard_map.148 = (bf16[640,3584]{1,0:T(8,128)(2,1)}, f32[640,3584]{1,0:T(8,128)}, f32[640,3584]{1,0:T(8,128)}, f32[256,1792]{1,0:T(8,128)S(1)}) custom-call(bf16[640,512]{1,0:T(8,128)(2,1)S(1)} %fusion.45.refs_0_, s32[512,1]{1,0:T(8,128)S(1)} %copy.23.refs_1_, ...), custom_call_target="tpu_custom_call", output_to_operand_aliasing={{0}: (8, {}), {1}: (9, {}), {2}: (10, {})} | custom-call | flops 1761607680 | bytes 22937600 | tf_op jit(solution)/shard_map/pallas_call | solution.py:93
  107.5 2.3 %fusion.97 = (f16[128,1792]{1,0:T(8,128)(2,1)S(1)}, f32[128,1792]{1,0:T(8,128)S(1)}) fusion(f32[256,1792]{1,0:T(8,128)S(1)} %get-tuple-element.72, f16[256,1792]{1,0:T(8,128)(2,1)} %collective-permute-done.13, s32[1792]{0:T(1024)S(1)} %get-tuple-element.101, f32[128]{0:T(128)S(1)} %copy-done.11, s32[128]{0:T(128)S(1)} %copy-done.7, f32[128]{0:T(128)S(1)} %copy-done.9, ...), kind=kLoop, calls=%fused_computation.129 | loop fusion | flops 6651904 | bytes 4137984 | tf_op jit(solution)/shard_map/convert_element_type | solution.py:305
  109.9 1.6 %collective-permute-start.18 = (f16[128,1792]{1,0:T(8,128)(2,1)S(1)}, f16[128,1792]{1,0:T(8,128)(2,1)S(1)}, u32[]{:S(2)}, u32[]{:S(2)}) collective-permute-start(f16[128,1792]{1,0:T(8,128)(2,1)S(1)} %get-tuple-element.111), channel_id=1, source_target_pairs={{0,2},{1,3},{2,0},{3,1},{4,6},{5,7},{6,4},{7,5},{8,10},{9,11},{10,... | collective-permute-start | bytes 1376264 | tf_op jit(solution)/shard_map/ppermute | solution.py:184
  111.5 1.0 add_convert_fusion.1
  112.5 0.4 collective-permute-start.14
  112.9 1.0 add_convert_fusion
  113.9 2.7 %collective-permute-start.16 = (f16[64,1792]{1,0:T(8,128)(2,1)S(1)}, f16[64,1792]{1,0:T(8,128)(2,1)S(1)}, u32[]{:S(2)}, u32[]{:S(2)}) collective-permute-start(f16[64,1792]{1,0:T(8,128)(2,1)S(1)} %add_convert_fusion), channel_id=1, source_target_pairs={{0,4},{1,5},{2,6},{3,7},{4,0},{5,1},{6,2},{7,3},{8,12},{9,13},{10,... | collective-permute-start | bytes 688136 | tf_op jit(solution)/shard_map/ppermute | solution.py:184
  116.6 1.0 fusion.117
  117.6 19.1 %collective-permute-done.14 = f16[64,1792]{1,0:T(8,128)(2,1)S(1)} collective-permute-done((f16[64,1792]{1,0:T(8,128)(2,1)S(1)}, f16[64,1792]{1,0:T(8,128)(2,1)S(1)}, u32[]{:S(2)}, u32[]{:S(2)}) %collective-permute-start.14) | collective-permute-done | bytes 229408 | tf_op jit(solution)/shard_map/ppermute | solution.py:184
  136.7 1.0 convert_add_fusion.1
  138.0 3.3 %collective-permute-done.16 = f16[64,1792]{1,0:T(8,128)(2,1)S(1)} collective-permute-done((f16[64,1792]{1,0:T(8,128)(2,1)S(1)}, f16[64,1792]{1,0:T(8,128)(2,1)S(1)}, u32[]{:S(2)}, u32[]{:S(2)}) %collective-permute-start.16) | collective-permute-done | bytes 229408 | tf_op jit(solution)/shard_map/ppermute | solution.py:184
  141.2 1.0 convert_add_fusion
  142.3 2.6 %collective-permute-done.19 = f16[64,1792]{1,0:T(8,128)(2,1)S(1)} collective-permute-done((f16[64,1792]{1,0:T(8,128)(2,1)S(1)}, f16[64,1792]{1,0:T(8,128)(2,1)S(1)}, u32[]{:S(2)}, u32[]{:S(2)}) %collective-permute-start.19) | collective-permute-done | bytes 229408 | tf_op jit(solution)/shard_map/ppermute | solution.py:184
  145.0 1.0 fusion.114
  (64 shorter events, 0.8 us)
Async XLA Ops:
  0.6 17.4 %copy-start = (bf16[128,640]{1,0:T(8,128)(2,1)S(1)}, bf16[128,640]{1,0:T(8,128)(2,1)}, u32[]{:S(2)}) copy-start(bf16[128,640]{1,0:T(8,128)(2,1)} %refs_0_.1) | copy-start | bytes 491524
  0.6 17.4 %collective-permute-start.4 = (bf16[128,640]{1,0:T(8,128)(2,1)}, bf16[128,640]{1,0:T(8,128)(2,1)S(1)}, u32[]{:S(2)}, u32[]{:S(2)}) collective-permute-start(bf16[128,640]{1,0:T(8,128)(2,1)} %refs_0_.1), channel_id=1, source_target_pairs={{0,16},{8,24},{16,0},{24,8},{1,17},{9,25},{17,1},{25,9},{2,18},{10... | collective-permute-start | bytes 491528 | tf_op jit(solution)/shard_map/ppermute | solution.py:194
  3.6 14.4 %collective-permute-start.3 = (bf16[128,640]{1,0:T(8,128)(2,1)}, bf16[128,640]{1,0:T(8,128)(2,1)S(1)}, u32[]{:S(2)}, u32[]{:S(2)}) collective-permute-start(bf16[128,640]{1,0:T(8,128)(2,1)} %refs_0_.1), channel_id=1, source_target_pairs={{0,8},{8,0},{16,24},{24,16},{1,9},{9,1},{17,25},{25,17},{2,10},{10... | collective-permute-start | bytes 491528 | tf_op jit(solution)/shard_map/ppermute | solution.py:194
  3.6 14.4 %collective-permute-start.5 = (bf16[128,640]{1,0:T(8,128)(2,1)}, bf16[128,640]{1,0:T(8,128)(2,1)S(1)}, u32[]{:S(2)}, u32[]{:S(2)}) collective-permute-start(bf16[128,640]{1,0:T(8,128)(2,1)} %refs_0_.1), channel_id=1, source_target_pairs={{0,24},{8,16},{16,8},{24,0},{1,25},{9,17},{17,9},{25,1},{2,26},{10... | collective-permute-start | bytes 491528 | tf_op jit(solution)/shard_map/ppermute | solution.py:194
  4.7 4.4 %collective-permute-start = (f32[512]{0:T(512)S(1)}, f32[512]{0:T(512)S(1)}, u32[]{:S(2)}, u32[]{:S(2)}) collective-permute-start(f32[512]{0:T(512)S(1)} %dynamic_update_slice.5), channel_id=1, source_target_pairs={{0,1},{1,0},{2,3},{3,2},{4,5},{5,4},{6,7},{7,6},{8,9},{9,8},{10,11... | collective-permute-start | bytes 6152 | tf_op jit(solution)/shard_map/ppermute | solution.py:184
  10.0 3.6 %collective-permute-start.1 = (f32[512]{0:T(512)S(1)}, f32[512]{0:T(512)S(1)}, u32[]{:S(2)}, u32[]{:S(2)}) collective-permute-start(f32[512]{0:T(512)S(1)} %add_dynamic-update-slice_fusion), channel_id=1, source_target_pairs={{0,2},{1,3},{2,0},{3,1},{4,6},{5,7},{6,4},{7,5},{8,10},{9,11},{10,... | collective-permute-start | bytes 6152 | tf_op jit(solution)/shard_map/ppermute | solution.py:184
  13.5 4.5 %collective-permute-start.2 = (f32[512]{0:T(512)S(1)}, f32[512]{0:T(512)S(1)}, u32[]{:S(2)}, u32[]{:S(2)}) collective-permute-start(f32[512]{0:T(512)S(1)} %add.489), channel_id=1, source_target_pairs={{0,4},{1,5},{2,6},{3,7},{4,0},{5,1},{6,2},{7,3},{8,12},{9,13},{10,... | collective-permute-start | bytes 6152 | tf_op jit(solution)/shard_map/ppermute | solution.py:184
  20.5 68.3 %copy-start.6 = (s32[128]{0:T(128)}, s32[128]{0:T(128)S(1)}, u32[]{:S(2)}) copy-start(s32[128]{0:T(128)S(1)} %get-tuple-element.98) | copy-start | bytes 1540
  20.9 51.8 %copy-start.8 = (f32[128]{0:T(128)}, f32[128]{0:T(128)S(1)}, u32[]{:S(2)}) copy-start(f32[128]{0:T(128)S(1)} %get-tuple-element.94) | copy-start | bytes 1540
  20.9 51.8 %copy-start.10 = (f32[128]{0:T(128)}, f32[128]{0:T(128)S(1)}, u32[]{:S(2)}) copy-start(f32[128]{0:T(128)S(1)} %get-tuple-element.96) | copy-start | bytes 1540
  21.2 6.2 %slice-start = ((s8[4587520]{0:T(1024)(128)(4,1)}), s8[4194304]{0:T(1024)(128)(4,1)S(1)}, s32[]{:S(2)}) async-start(s8[4587520]{0:T(1024)(128)(4,1)} %bitcast.6), calls=%async_computation | async-start | bytes 8388608
  21.3 11.9 %collective-permute-start.6 = (f32[512]{0:T(512)S(1)}, f32[512]{0:T(512)S(1)}, u32[]{:S(2)}, u32[]{:S(2)}) collective-permute-start(f32[512]{0:T(512)S(1)} %add.490), channel_id=1, source_target_pairs={{0,8},{8,0},{16,24},{24,16},{1,9},{9,1},{17,25},{25,17},{2,10},{10... | collective-permute-start | bytes 6152 | tf_op jit(solution)/shard_map/ppermute | solution.py:184
  21.4 3.9 %copy-start.1 = (bf16[640,3584]{1,0:T(8,128)(2,1)S(1)}, bf16[640,3584]{1,0:T(8,128)(2,1)}, u32[]{:S(2)}) copy-start(bf16[640,3584]{1,0:T(8,128)(2,1)} %refs_5_.7) | copy-start | bytes 13762564
  21.4 6.0 %slice-start.1 = ((s8[4587520]{0:T(1024)(128)(4,1)}), s8[393216]{0:T(1024)(128)(4,1)S(1)}, s32[]{:S(2)}) async-start(s8[4587520]{0:T(1024)(128)(4,1)} %bitcast.6), calls=%async_computation.1 | async-start | bytes 786432
  29.6 59.2 %collective-permute-start.11 = (f16[256,1792]{1,0:T(8,128)(2,1)}, f16[256,1792]{1,0:T(8,128)(2,1)}, u32[]{:S(2)}, u32[]{:S(2)}) collective-permute-start(f16[256,1792]{1,0:T(8,128)(2,1)} %fusion.2), channel_id=1, source_target_pairs={{0,1},{1,0},{2,3},{3,2},{4,5},{5,4},{6,7},{7,6},{8,9},{9,8},{10,11... | collective-permute-start | bytes 2752520 | tf_op jit(solution)/shard_map/ppermute | solution.py:184
  30.8 42.0 %collective-permute-start.10 = (f16[256,1792]{1,0:T(8,128)(2,1)}, f16[256,1792]{1,0:T(8,128)(2,1)}, u32[]{:S(2)}, u32[]{:S(2)}) collective-permute-start(f16[256,1792]{1,0:T(8,128)(2,1)} %fusion.1), channel_id=1, source_target_pairs={{0,1},{1,0},{2,3},{3,2},{4,5},{5,4},{6,7},{7,6},{8,9},{9,8},{10,11... | collective-permute-start | bytes 2752520 | tf_op jit(solution)/shard_map/ppermute | solution.py:184
  31.7 31.3 %collective-permute-start.8 = (f16[256,1792]{1,0:T(8,128)(2,1)}, f16[256,1792]{1,0:T(8,128)(2,1)S(1)}, u32[]{:S(2)}, u32[]{:S(2)}) collective-permute-start(f16[256,1792]{1,0:T(8,128)(2,1)} %fusion), channel_id=1, source_target_pairs={{0,2},{1,3},{2,0},{3,1},{4,6},{5,7},{6,4},{7,5},{8,10},{9,11},{10,... | collective-permute-start | bytes 2752520 | tf_op jit(solution)/shard_map/ppermute | solution.py:184
  33.3 4.7 %collective-permute-start.7 = (f32[512]{0:T(512)S(1)}, f32[512]{0:T(512)S(1)}, u32[]{:S(2)}, u32[]{:S(2)}) collective-permute-start(f32[512]{0:T(512)S(1)} %add.499), channel_id=1, source_target_pairs={{0,16},{8,24},{16,0},{24,8},{1,17},{9,25},{17,1},{25,9},{2,18},{10... | collective-permute-start | bytes 6152 | tf_op jit(solution)/shard_map/ppermute | solution.py:184
  36.8 70.6 %collective-permute-start.13 = (f16[256,1792]{1,0:T(8,128)(2,1)}, f16[256,1792]{1,0:T(8,128)(2,1)}, u32[]{:S(2)}, u32[]{:S(2)}) collective-permute-start(f16[256,1792]{1,0:T(8,128)(2,1)} %fusion.3), channel_id=1, source_target_pairs={{0,1},{1,0},{2,3},{3,2},{4,5},{5,4},{6,7},{7,6},{8,9},{9,8},{10,11... | collective-permute-start | bytes 2752520 | tf_op jit(solution)/shard_map/ppermute | solution.py:184
  63.0 1.0 copy-start.5
  66.7 40.7 %collective-permute-start.9 = (f16[128,1792]{1,0:T(8,128)(2,1)}, f16[128,1792]{1,0:T(8,128)(2,1)}, u32[]{:S(2)}, u32[]{:S(2)}) collective-permute-start(f16[128,1792]{1,0:T(8,128)(2,1)} %get-tuple-element.108), channel_id=1, source_target_pairs={{0,1},{1,0},{2,3},{3,2},{4,5},{5,4},{6,7},{7,6},{8,9},{9,8},{10,11... | collective-permute-start | bytes 1376264 | tf_op jit(solution)/shard_map/ppermute | solution.py:184
  76.0 16.5 %collective-permute-start.12 = (f16[128,1792]{1,0:T(8,128)(2,1)}, f16[128,1792]{1,0:T(8,128)(2,1)}, u32[]{:S(2)}, u32[]{:S(2)}) collective-permute-start(f16[128,1792]{1,0:T(8,128)(2,1)} %get-tuple-element.114), channel_id=1, source_target_pairs={{0,2},{1,3},{2,0},{3,1},{4,6},{5,7},{6,4},{7,5},{8,10},{9,11},{10,... | collective-permute-start | bytes 1376264 | tf_op jit(solution)/shard_map/ppermute | solution.py:184
  88.8 3.7 %copy-start.2 = (f32[128,1792]{1,0:T(8,128)S(1)}, f32[128,1792]{1,0:T(8,128)}, u32[]{:S(2)}) copy-start(f32[128,1792]{1,0:T(8,128)} %get-tuple-element.113) | copy-start | bytes 2752516
  92.1 20.8 %collective-permute-start.15 = (f16[128,1792]{1,0:T(8,128)(2,1)S(1)}, f16[128,1792]{1,0:T(8,128)(2,1)}, u32[]{:S(2)}, u32[]{:S(2)}) collective-permute-start(f16[128,1792]{1,0:T(8,128)(2,1)S(1)} %get-tuple-element.110), channel_id=1, source_target_pairs={{0,2},{1,3},{2,0},{3,1},{4,6},{5,7},{6,4},{7,5},{8,10},{9,11},{10,... | collective-permute-start | bytes 1376264 | tf_op jit(solution)/shard_map/ppermute | solution.py:184
  93.5 23.0 %collective-permute-start.17 = (f16[64,1792]{1,0:T(8,128)(2,1)S(1)}, f16[64,1792]{1,0:T(8,128)(2,1)S(1)}, u32[]{:S(2)}, u32[]{:S(2)}) collective-permute-start(f16[64,1792]{1,0:T(8,128)(2,1)S(1)} %fusion.118), channel_id=1, source_target_pairs={{0,4},{1,5},{2,6},{3,7},{4,0},{5,1},{6,2},{7,3},{8,12},{9,13},{10,... | collective-permute-start | bytes 688136 | tf_op jit(solution)/shard_map/ppermute | solution.py:184
  96.3 11.1 %copy-start.7 = (s32[128]{0:T(128)S(1)}, s32[128]{0:T(128)}, u32[]{:S(2)}) copy-start(s32[128]{0:T(128)} %copy-done.6) | copy-start | bytes 1540
  96.3 11.1 %copy-start.9 = (f32[128]{0:T(128)S(1)}, f32[128]{0:T(128)}, u32[]{:S(2)}) copy-start(f32[128]{0:T(128)} %copy-done.8) | copy-start | bytes 1540
  96.4 11.1 %copy-start.11 = (f32[128]{0:T(128)S(1)}, f32[128]{0:T(128)}, u32[]{:S(2)}) copy-start(f32[128]{0:T(128)} %copy-done.10) | copy-start | bytes 1540
  107.5 5.4 %copy-start.4 = (f32[128,1792]{1,0:T(8,128)S(1)}, f32[128,1792]{1,0:T(8,128)}, u32[]{:S(2)}) copy-start(f32[128,1792]{1,0:T(8,128)} %get-tuple-element.81) | copy-start | bytes 2752516
  109.8 6.7 %copy-start.3 = (f32[128,1792]{1,0:T(8,128)S(1)}, f32[128,1792]{1,0:T(8,128)}, u32[]{:S(2)}) copy-start(f32[128,1792]{1,0:T(8,128)} %get-tuple-element.113) | copy-start | bytes 2752516
  109.9 27.9 %collective-permute-start.18 = (f16[128,1792]{1,0:T(8,128)(2,1)S(1)}, f16[128,1792]{1,0:T(8,128)(2,1)S(1)}, u32[]{:S(2)}, u32[]{:S(2)}) collective-permute-start(f16[128,1792]{1,0:T(8,128)(2,1)S(1)} %get-tuple-element.111), channel_id=1, source_target_pairs={{0,2},{1,3},{2,0},{3,1},{4,6},{5,7},{6,4},{7,5},{8,10},{9,11},{10,... | collective-permute-start | bytes 1376264 | tf_op jit(solution)/shard_map/ppermute | solution.py:184
  112.5 24.3 %collective-permute-start.14 = (f16[64,1792]{1,0:T(8,128)(2,1)S(1)}, f16[64,1792]{1,0:T(8,128)(2,1)S(1)}, u32[]{:S(2)}, u32[]{:S(2)}) collective-permute-start(f16[64,1792]{1,0:T(8,128)(2,1)S(1)} %add_convert_fusion.1), channel_id=1, source_target_pairs={{0,4},{1,5},{2,6},{3,7},{4,0},{5,1},{6,2},{7,3},{8,12},{9,13},{10,... | collective-permute-start | bytes 688136 | tf_op jit(solution)/shard_map/ppermute | solution.py:184
  113.9 27.3 %collective-permute-start.16 = (f16[64,1792]{1,0:T(8,128)(2,1)S(1)}, f16[64,1792]{1,0:T(8,128)(2,1)S(1)}, u32[]{:S(2)}, u32[]{:S(2)}) collective-permute-start(f16[64,1792]{1,0:T(8,128)(2,1)S(1)} %add_convert_fusion), channel_id=1, source_target_pairs={{0,4},{1,5},{2,6},{3,7},{4,0},{5,1},{6,2},{7,3},{8,12},{9,13},{10,... | collective-permute-start | bytes 688136 | tf_op jit(solution)/shard_map/ppermute | solution.py:184
  137.9 7.0 %collective-permute-start.19 = (f16[64,1792]{1,0:T(8,128)(2,1)S(1)}, f16[64,1792]{1,0:T(8,128)(2,1)S(1)}, u32[]{:S(2)}, u32[]{:S(2)}) collective-permute-start(f16[64,1792]{1,0:T(8,128)(2,1)S(1)} %fusion.115), channel_id=1, source_target_pairs={{0,4},{1,5},{2,6},{3,7},{4,0},{5,1},{6,2},{7,3},{8,12},{9,13},{10,... | collective-permute-start | bytes 688136 | tf_op jit(solution)/shard_map/ppermute | solution.py:184

commit v2 on v1

v2 whole, which is shorter than its diff:
```python
import functools

import jax
import jax.numpy as jnp
from jax import lax
from jax.experimental import pallas as pl
from jax.experimental.pallas import tpu as pltpu
from jax.sharding import PartitionSpec as P

noise_scale = 0.01
learn_rate = 0.002
beta_first = 0.9
beta_second = 0.99
adam_floor = 1e-08
stat_epsilon = 1e-06

f32 = jnp.float32
bf16 = jnp.bfloat16
wire = jnp.float16


def mixed_levels(mixed):
    mixed = jnp.bitwise_xor(mixed, jnp.right_shift(mixed, 15))
    mixed = mixed * 73244475
    mixed = jnp.bitwise_xor(mixed, jnp.right_shift(mixed, 13))
    level = jnp.bitwise_and(mixed, 255)
    return level.astype(f32) * (2.0 / 256.0) - 255.0 / 256.0


def member_part(seeds):
    return seeds * 1103515245


def column_part(columns, salt):
    return columns * 40503 + salt * 7919


def factor_levels(seed, column, salt):
    return mixed_levels(member_part(seed) + column_part(column, salt))


def factor_block(seeds, start, count, salt):
    columns = jnp.arange(count, dtype=jnp.int32) + start
    return factor_levels(seeds[:, None], columns[None, :], salt)


def factor_block_turned(seeds, start, count, salt):
    columns = jnp.arange(count, dtype=jnp.int32) + start
    return factor_levels(seeds[None, :], columns[:, None], salt).astype(bf16)


def adam_kernel(scale, row_tile, keeps, extra, *refs):
    left, member, unit, scaled, weight, first, second = refs[:7]
    if keeps:
        tokens, along, kept_member = refs[7:10]
    outs = refs[7 + 3 * keeps + extra :]
    weight_new, first_new, second_new, tick = outs[:4]
    tick[...] = jnp.zeros_like(tick)
    weighted = (scaled[...] * mixed_levels(member[...] + unit[...])).astype(bf16)
    if keeps:
        product = jnp.dot(tokens[...], weight[...], preferred_element_type=f32)
        outs[4][...] = product + along[...] * mixed_levels(kept_member[...] + unit[...])
    for start in range(0, left.shape[0], row_tile):
        rows = slice(start, start + row_tile)
        g = jnp.dot(left[rows, :], weighted, preferred_element_type=f32)
        f = beta_first * first[rows, :] + ((1.0 - beta_first) * scale) * g
        s = beta_second * second[rows, :] + ((1.0 - beta_second) * scale * scale) * g * g
        first_new[rows, :] = f
        second_new[rows, :] = s
        floor = s * lax.rsqrt(s) + adam_floor
        inverse = pl.reciprocal(floor, approx=True)
        inverse = inverse * (2.0 - floor * inverse)
        moved = weight[rows, :].astype(f32) + (learn_rate * f) * inverse
        weight_new[rows, :] = moved.astype(bf16)


def adam_part(left, member, unit, scaled, weight, first, second, kept_from, before, wait_for, start, size):
    width, units = weight.shape
    members = member.shape[0]
    tile = max(t for t in range(128, 1281, 128) if size % t == 0 and start % t == 0)
    base = start // tile
    keeps = kept_from is not None
    full = lambda dtype: jax.ShapeDtypeStruct((width, units), dtype)
    big = lambda: pl.BlockSpec((width, tile), lambda j: (0, base + j))
    fixed = lambda x: pl.BlockSpec(x.shape, lambda j: (0, 0))
    in_specs = [
        fixed(left),
        fixed(member),
        pl.BlockSpec((1, tile), lambda j: (0, base + j)),
        fixed(scaled),
        big(),
        big(),
        big(),
    ]
    args = [left, member, unit, scaled, weight, first, second]
    out_specs = [big(), big(), big(), pl.BlockSpec((1, 1), lambda j: (0, 0))]
    out_shape = [full(bf16), full(f32), full(f32), jax.ShapeDtypeStruct((1, 1), f32)]
    kept_rows = 0
    if keeps:
        kept_rows = kept_from[0].shape[0]
        in_specs += [fixed(x) for x in kept_from]
        args += list(kept_from)
        out_specs.append(pl.BlockSpec((kept_rows, tile), lambda j: (0, j)))
        out_shape.append(jax.ShapeDtypeStruct((kept_rows, size), f32))
    aliases = {}
    if before is not None:
        aliases = {len(args) + i: i for i in range(len(before))}
        args += list(before)
    args += list(wait_for)
    extra = len(args) - len(in_specs)
    in_specs += [pl.BlockSpec(memory_space=pl.ANY)] * extra
    return pl.pallas_call(
        functools.partial(adam_kernel, 1.0 / (members * noise_scale), width // 2, keeps, extra),
        grid=(size // tile,),
        in_specs=in_specs,
        out_specs=out_specs,
        out_shape=out_shape,
        input_output_aliases=aliases,
        compiler_params=pltpu.CompilerParams(vmem_limit_bytes=44 * 1024 * 1024),
        cost_estimate=pl.CostEstimate(
            flops=2 * width * size * (members + kept_rows),
            bytes_accessed=20 * width * size,
            transcendentals=0,
        ),
    )(*args)


def sort_kernel(orders, share, index, seeds, columns, *refs):
    kinds = len(orders)
    pieces = refs[: -3 * kinds - 1]
    turned, alongs, ids = (refs[len(pieces) + i * kinds :][:kinds] for i in range(3))
    held = refs[-1]
    per_piece = pieces[0].shape[0] // share
    for p, piece in enumerate(pieces):
        for k in range(per_piece):
            held[p * per_piece + k] = piece[k * share : (k + 1) * share, :]
    for mask in range(held.shape[0]):
        rows = held[index[0, mask]]
        block = pl.multiple_of(index[1, mask] * share, share)
        member = member_part(seeds[pl.ds(block, share), :])
        wide = rows.astype(f32)
        along = [
            noise_scale
            * jnp.sum(wide * mixed_levels(member + columns[i : i + 1, :]), axis=1, keepdims=True)
            for i in range(2)
        ]
        for kind, order in enumerate(orders):
            at = order.index(mask) * share
            turned[kind][at : at + share, :] = rows
            ids[kind][at : at + share, :] = member
            for i in range(2):
                alongs[kind][at : at + share, i : i + 1] = along[i]


def sort_blocks(pieces, index, seeds, columns, orders):
    members = seeds.shape[0]
    width = pieces[0].shape[1]
    shares = len(orders[0])
    share = members // shares
    kinds = len(orders)
    whole = pl.BlockSpec(memory_space=pltpu.VMEM)
    outs = pl.pallas_call(
        functools.partial(sort_kernel, orders, share),
        in_specs=[pl.BlockSpec(memory_space=pltpu.SMEM)] + [whole] * (2 + len(pieces)),
        out_specs=[whole] * (3 * kinds),
        out_shape=[jax.ShapeDtypeStruct((members, width), bf16)] * kinds
        + [jax.ShapeDtypeStruct((members, 2), f32)] * kinds
        + [jax.ShapeDtypeStruct((members, 1), jnp.int32)] * kinds,
        scratch_shapes=[pltpu.VMEM((shares, share, width), bf16)],
        compiler_params=pltpu.CompilerParams(vmem_limit_bytes=32 * 1024 * 1024),
    )(index, seeds[:, None], columns, *pieces)
    return outs[:kinds], outs[kinds : 2 * kinds], outs[2 * kinds :]


def block_order(bits):
    order = [0]
    for bit in reversed(bits):
        order = order + [mask ^ (1 << bit) for mask in order]
    return order


def shards(
    tokens, seeds, fitness, gate_weight, up_weight, gate_first, up_first, gate_second, up_second
):
    members = seeds.shape[0]
    width_part, unit_part = gate_weight.shape
    shares = lax.axis_size("fsdp")
    share = members // shares
    me = lax.axis_index("fsdp")
    width_start = me * width_part
    unit_start = lax.axis_index("pop") * unit_part
    levels = shares.bit_length() - 1
    across = list(range(levels))
    along_first = [1, 0] + across[2:] if levels > 1 else across

    def exchange(x, mask, axis="fsdp"):
        size = lax.axis_size(axis)
        return lax.ppermute(x, axis, [(i, i ^ mask) for i in range(size)])

    pops = lax.axis_size("pop")
    pop = lax.axis_index("pop")
    per_pop = shares // pops
    pieces = [tokens]
    for mask in reversed(range(1, pops)):
        pieces.insert(1, exchange(tokens, mask, "pop"))

    group = members // fitness.shape[0]
    own = jnp.arange(group)[:, None] == pop * shares + me
    fit = jnp.where(own, fitness[None, :], 0.0)
    turned_gate = factor_block_turned(seeds, width_start, width_part, 1)
    fit = fit + exchange(fit, 1)
    turned_up = factor_block_turned(seeds, width_start, width_part, 3)
    for bit in range(1, levels - 1):
        fit = fit + exchange(fit, 1 << bit)

    masks = jnp.arange(shares)
    blocks = jnp.bitwise_xor(me, masks)
    slots = jnp.bitwise_xor(blocks // per_pop, pop) * per_pop + blocks % per_pop
    features = jnp.arange(width_part, dtype=jnp.int32) + width_start
    orders = [block_order(across), block_order(along_first)]
    bits_of = [across, along_first]
    tokens_of, along_of, member_of = sort_blocks(
        pieces,
        jnp.stack([slots, blocks]).astype(jnp.int32),
        seeds,
        jnp.stack([column_part(features, 1), column_part(features, 3)]),
        orders,
    )

    columns = jnp.arange(unit_part, dtype=jnp.int32) + unit_start
    member = member_part(seeds)[:, None]

    half = members // 2
    unit_tiles = unit_part // 128
    cut = {"gate": unit_tiles // 2 * 128, "up": unit_tiles // 2 * 128}
    plan = [("gate", 0, 1), ("up", 0, 0), ("gate", 1, 0), ("up", 1, 1)]

    def span(index):
        name, at, _ = plan[index]
        return (0, cut[name]) if at == 0 else (cut[name], unit_part)

    state = {
        "gate": (turned_gate, column_part(columns, 2)[None, :], gate_weight, gate_first, gate_second),
        "up": (turned_up, column_part(columns, 4)[None, :], up_weight, up_first, up_second),
    }

    def product(index, rows, tick):
        name, _, kind = plan[index]
        start, stop = span(index)
        total = jnp.dot(
            tokens_of[kind][rows], state[name][2][:, start:stop], preferred_element_type=f32
        )
        along = along_of[kind][rows, {"gate": 0, "up": 1}[name]][:, None]
        if tick is not None:
            along = along + tick
        unit = state[name][1][:, start:stop]
        return total + along * mixed_levels(member_of[kind][rows] + unit)

    sent = [None] * len(plan)

    def zero_of(x):
        return x[:1, :1].astype(f32) * 0.0

    def send(index, tick):
        partial = product(index, slice(half, None), tick).astype(wire)
        sent[index] = exchange(partial, 1 << bits_of[plan[index][2]][0])
        return partial

    fit = fit + zero_of(along_of[0])
    if levels > 1:
        fit = fit + exchange(fit, 1 << (levels - 1))
    ready = fit[:1, :1] * 0.0
    wait = [send(1, None), send(0, ready), send(2, ready)]
    wait = [x[:8, :128].astype(f32) for x in wait]
    fit = sum([exchange(fit, mask, "pop") for mask in range(1, pops)], fit)
    center = jnp.mean(fit)
    spread = jnp.mean(jnp.square(fit - center))
    scaled = ((fit - center) / jnp.sqrt(spread + stat_epsilon)).reshape(members, 1)

    updated = {"gate": None, "up": None}
    kept_of = {}
    summed = {}
    running = {}

    def update(index, wait_for=(), keeps=True, piece=0, pieces=1):
        name, _, kind = plan[index]
        left, unit, weight, first, second = state[name]
        start, stop = span(index)
        size = (stop - start) // pieces
        start += piece * size
        kept_from = None
        if keeps:
            side = {"gate": 0, "up": 1}[name]
            kept_from = (
                tokens_of[kind][:half],
                along_of[kind][:half, side : side + 1],
                member_of[kind][:half],
            )
        done = adam_part(
            left,
            member,
            unit,
            scaled,
            weight,
            first,
            second,
            kept_from,
            updated[name],
            wait_for,
            start,
            size,
        )
        updated[name] = done[:3]
        if keeps:
            kept_of[index] = done[4]
        return done[3]

    def reduce_step(index, level, tick):
        if level == 0:
            running[index] = [kept_of[index], sent[index]]
        kept, arrived = running[index]
        rows = arrived.shape[0] // 2
        if level == levels - 1:
            summed[index] = kept + arrived.astype(f32) + tick
            return summed[index]
        added = lambda part: kept[part] + arrived[part].astype(f32) + tick
        outgoing = added(slice(rows, 2 * rows)).astype(wire)
        bit = bits_of[plan[index][2]][level + 1]
        running[index] = [added(slice(0, rows)), exchange(outgoing, 1 << bit)]
        return running[index][0]

    tick = update(0, wait)
    wait = [reduce_step(0, 0, tick)]
    kept_of[1] = product(1, slice(0, half), tick)
    wait += [reduce_step(1, 0, tick), send(3, tick)[:8, :128].astype(f32)]
    tick = update(1, wait, keeps=False)
    wait = [reduce_step(1, 1, tick), reduce_step(0, 1, tick)]
    for index in (2, 3):
        kept_of[index] = product(index, slice(0, half), tick)
        wait.append(reduce_step(index, 0, tick))
    tick = update(2, wait, keeps=False)
    wait = [reduce_step(2, 1, tick), reduce_step(3, 1, tick)]
    tick = update(3, wait, keeps=False)
    for level in range(2, levels):
        for index in (0, 1, 2, 3):
            reduce_step(index, level, tick)

    def finished(name):
        return jnp.concatenate([summed[i] for i in range(len(plan)) if plan[i][0] == name], axis=1)

    hidden = (jax.nn.silu(finished("gate")) * finished("up")).astype(bf16)
    gate_new, gate_first_new, gate_second_new = updated["gate"]
    up_new, up_first_new, up_second_new = updated["up"]
    return (hidden, gate_new, up_new, gate_first_new, up_first_new, gate_second_new, up_second_new)


def solution(mesh):
    placed = (P("pop", "fsdp"), P(), P(("pop", "fsdp"))) + (P("fsdp", "pop"),) * 6
    return jax.shard_map(
        shards,
        mesh=mesh,
        in_specs=placed,
        out_specs=(P("fsdp", "pop"),) * 7,
        check_vma=False,
    )
```

time: 146 us -> 132 us (0.904); the launches traced: 146 us -> 131 us
  waiting for transfers between devices: 32.9 us -> 10.8 us
  Pallas kernels: 46.7 us -> 41.8 us
  other arithmetic: 24.1 us -> 27.7 us
  matrix products: 10.1 us -> 12.9 us
  starting transfers between devices: 26.1 us -> 28 us
  local copies, waits for them, and re-layouts: 3.84 us -> 5.66 us
    ppermute x20 -> x21, waiting for transfers between devices: 32.9 us -> 10.8 us  [exchange(): return lax.ppermute(x, axis, [(i, i ^ mask) for i in range(size)])]
    convert_element_type x5 -> x8, other arithmetic: 5.4 us -> 13.8 us  [reduce_step(): outgoing = added(slice(rows, 2 * rows)).astype(wire)]
    add x11 -> x13, other arithmetic: 13.3 us -> 6.4 us  [the longest x6 3.4 us: product(): along = along + tick]
    pallas_call x4, Pallas kernels: 44.5 us -> 39.7 us  [adam_part(): pl.pallas_call(functools.partial(adam_kernel, 1.0 / (members * noise_scal...]
    dot_general x4 -> x7, matrix products: 10.1 us -> 12.9 us  [product(): jnp.dot(tokens_of[kind][rows], state[name][2][:, start:stop], preferred_e...]
    convert_element_type x0 -> x4, other arithmetic: none -> 2.72 us  [the longest x3 2.05 us: shards(): wait = [x[:8, :128].astype(f32) for x in wait]]
    ppermute x20 -> x21, starting transfers between devices: 26.1 us -> 28 us  [exchange(): return lax.ppermute(x, axis, [(i, i ^ mask) for i in range(size)])]
    slice x7 -> x6, local copies, waits for them, and re-layouts: 0.55 us -> 2.13 us  [the longest x2 0.67 us: product(): unit = state[name][1][:, start:stop]]
  transfers between devices with their start and end apart: 20 -> 21, of which waited for: 6 -> 4; matrix products, arithmetic and copies ran while one was open for 24% -> 32% of each run, Pallas kernels for 30% -> 32%
where the time goes in v2:
time: 132 us; the launch traced here: 131 us
  Pallas kernels  41.8 us (32%)
  starting transfers between devices  28 us (21%)
  other arithmetic  27.7 us (21%)
  matrix products  12.9 us (10%)
  waiting for transfers between devices  10.8 us (8%)
  local copies, waits for them, and re-layouts  5.66 us (4%)
  between operations  3.72 us (3%)
    pallas_call x4, Pallas kernels, adam_part(): pl.pallas_call(functools.partial(adam_kernel, 1.0 / (members * noise_scal...  39.7 us
    ppermute x21, starting transfers between devices, exchange(): return lax.ppermute(x, axis, [(i, i ^ mask) for i in range(size)])  28 us
    convert_element_type x8, other arithmetic, reduce_step(): outgoing = added(slice(rows, 2 * rows)).astype(wire)  13.8 us
    dot_general x7, matrix products, product(): jnp.dot(tokens_of[kind][rows], state[name][2][:, start:stop], preferred_e...  12.9 us
    ppermute x21, waiting for transfers between devices, exchange(): return lax.ppermute(x, axis, [(i, i ^ mask) for i in range(size)])  10.8 us
    add x6, other arithmetic, product(): along = along + tick  3.4 us
    add x4, other arithmetic, reduce_step(): summed[index] = kept + arrived.astype(f32) + tick  2.84 us
  transfers between devices with their start and end apart: 21, of which 4 were waited for; matrix products, arithmetic and copies ran while one was open for 32% of the time, Pallas kernels for 32%

profile of v2, /device:TPU:0, one launch (start us, length us, event | category | flops | bytes accessed | tf_op | source)
XLA Modules:
  0.0 130.5 jit_solution(1605632548010956146)
XLA Ops:
  0.7 3.0 %collective-permute-start.3 = (bf16[128,640]{1,0:T(8,128)(2,1)}, bf16[128,640]{1,0:T(8,128)(2,1)S(1)}, u32[]{:S(2)}, u32[]{:S(2)}) collective-permute-start(bf16[128,640]{1,0:T(8,128)(2,1)} %refs_0_.1), channel_id=1, source_target_pairs={{0,16},{8,24},{16,0},{24,8},{1,17},{9,25},{17,1},{25,9},{2,18},{10... | collective-permute-start | bytes 491528 | tf_op jit(solution)/shard_map/ppermute | solution.py:198
  3.9 0.7 broadcast_select_fusion
  4.6 2.0 %collective-permute-start = (f32[32,16]{1,0:T(8,128)S(1)}, f32[32,16]{1,0:T(8,128)S(1)}, u32[]{:S(2)}, u32[]{:S(2)}) collective-permute-start(f32[32,16]{1,0:T(8,128)S(1)} %broadcast_select_fusion), channel_id=1, source_target_pairs={{0,1},{1,0},{2,3},{3,2},{4,5},{5,4},{6,7},{7,6},{8,9},{9,8},{10,11... | collective-permute-start | bytes 6152 | tf_op jit(solution)/shard_map/ppermute | solution.py:198
  6.6 0.7 broadcast_multiply_fusion
  7.4 0.6 slice_reduce_fusion.5
  8.0 1.0 fusion.58
  9.2 0.8 copy.22.seeds
  10.1 1.6 %collective-permute-start.1 = (f32[32,16]{1,0:T(8,128)S(1)}, f32[32,16]{1,0:T(8,128)S(1)}, u32[]{:S(2)}, u32[]{:S(2)}) collective-permute-start(f32[32,16]{1,0:T(8,128)S(1)} %fusion.95), channel_id=1, source_target_pairs={{0,2},{1,3},{2,0},{3,1},{4,6},{5,7},{6,4},{7,5},{8,10},{9,11},{10,... | collective-permute-start | bytes 6152 | tf_op jit(solution)/shard_map/ppermute | solution.py:198
  11.7 2.1 %shard_map.144 = (bf16[512,640]{1,0:T(8,128)(2,1)S(1)}, bf16[512,640]{1,0:T(8,128)(2,1)S(1)}, f32[512,2]{1,0:T(8,128)S(1)}, f32[512,2]{1,0:T(8,128)S(1)}, s32[512,1]{1,0:T(8,128)S(1)}, /*index=5*/s32[512,1]{1,0:T(8,128)S(1)}) custom-call(s32[2,8]{1,0:T(2,128)S(1)} %pad_add_fusion.1.index, s32[512,1]{1,0:T(8,128)S(1)} %copy.22.seeds, ...), custom_call_target="tpu_custom_call" | custom-call | tf_op jit(solution)/shard_map/pallas_call | solution.py:162
  13.9 0.7 slice.200
  15.3 2.6 %collective-permute-start.5 = (f32[32,16]{1,0:T(8,128)S(1)}, f32[32,16]{1,0:T(8,128)S(1)}, u32[]{:S(2)}, u32[]{:S(2)}) collective-permute-start(f32[32,16]{1,0:T(8,128)S(1)} %add_add_fusion.6), channel_id=1, source_target_pairs={{0,4},{1,5},{2,6},{3,7},{4,0},{5,1},{6,2},{7,3},{8,12},{9,13},{10,... | collective-permute-start | bytes 6152 | tf_op jit(solution)/shard_map/ppermute | solution.py:198
  18.1 2.2 %collective-permute-done.5 = f32[32,16]{1,0:T(8,128)S(1)} collective-permute-done((f32[32,16]{1,0:T(8,128)S(1)}, f32[32,16]{1,0:T(8,128)S(1)}, u32[]{:S(2)}, u32[]{:S(2)}) %collective-permute-start.5) | collective-permute-done | bytes 2080 | tf_op jit(solution)/shard_map/ppermute | solution.py:198
  20.3 0.5 slice.264
  20.9 1.5 %collective-permute-start.7 = (f32[32,16]{1,0:T(8,128)S(1)}, f32[32,16]{1,0:T(8,128)S(1)}, u32[]{:S(2)}, u32[]{:S(2)}) collective-permute-start(f32[32,16]{1,0:T(8,128)S(1)} %add.608), channel_id=1, source_target_pairs={{0,16},{8,24},{16,0},{24,8},{1,17},{9,25},{17,1},{25,9},{2,18},{10... | collective-permute-start | bytes 6152 | tf_op jit(solution)/shard_map/ppermute | solution.py:198
  22.4 0.3 collective-permute-start.6
  23.6 3.8 %fusion = f16[256,1792]{1,0:T(8,128)(2,1)} fusion(bf16[640,3584]{1,0:T(8,128)(2,1)} %refs_4_.7, s32[1792]{0:T(1024)S(1)} %get-tuple-element.60, s32[256]{0:T(256)S(1)} %get-tuple-element.54, f32[256]{0:T(256)S(1)} %get-tuple-element.56, bf16[512,640]{1,0:T(8,128)(2,1)S(1)} %get-tuple-element.34), kind=kOutput, calls=%fused_computation.21 | convolution fusion | flops 593166336 | bytes 3549184 | tf_op jit(solution)/shard_map/dot_general | solution.py:250
  27.4 0.7 slice_convert_fusion.3.refs_10_
  28.1 0.4 collective-permute-start.11
  28.6 2.0 %fusion.2 = f16[256,1792]{1,0:T(8,128)(2,1)} fusion(bf16[640,3584]{1,0:T(8,128)(2,1)S(1)} %bitcast.9, s32[1792]{0:T(1024)S(1)} %get-tuple-element.61, f32[256]{0:T(256)S(1)} %get-tuple-element.55, s32[256]{0:T(256)S(1)} %get-tuple-element.54, bf16[512,640]{1,0:T(8,128)(2,1)S(1)} %get-tuple-element.34), kind=kOutput, calls=%fused_computation.23 | convolution fusion | flops 593166336 | bytes 3549184 | tf_op jit(solution)/shard_map/dot_general | solution.py:250
  30.6 0.7 slice_convert_fusion.1.refs_12_
  31.3 1.6 %collective-permute-start.13 = (f16[256,1792]{1,0:T(8,128)(2,1)}, f16[256,1792]{1,0:T(8,128)(2,1)}, u32[]{:S(2)}, u32[]{:S(2)}) collective-permute-start(f16[256,1792]{1,0:T(8,128)(2,1)} %fusion.2), channel_id=1, source_target_pairs={{0,1},{1,0},{2,3},{3,2},{4,5},{5,4},{6,7},{7,6},{8,9},{9,8},{10,11... | collective-permute-start | bytes 2752520 | tf_op jit(solution)/shard_map/ppermute | solution.py:198
  33.0 2.1 %fusion.1 = f16[256,1792]{1,0:T(8,128)(2,1)} fusion(bf16[640,3584]{1,0:T(8,128)(2,1)S(1)} %bitcast.9, s32[1792]{0:T(1024)S(1)} %copy-done.8, s32[256]{0:T(256)S(1)} %get-tuple-element.57, f32[256]{0:T(256)S(1)} %get-tuple-element.81, bf16[512,640]{1,0:T(8,128)(2,1)S(1)} %get-tuple-element.31), kind=kOutput, calls=%fused_computation.22 | convolution fusion | flops 593166336 | bytes 3549184 | tf_op jit(solution)/shard_map/dot_general | solution.py:250
  35.1 0.7 slice_convert_fusion.2.refs_11_
  35.8 0.5 collective-permute-start.9
  36.3 0.6 fusion.102
  37.5 0.6 multiply_reduce_fusion
  39.0 2.3 %copy-done = bf16[640,3584]{1,0:T(8,128)(2,1)S(1)} copy-done((bf16[640,3584]{1,0:T(8,128)(2,1)S(1)}, bf16[640,3584]{1,0:T(8,128)(2,1)}, u32[]{:S(2)}) %copy-start) | copy-done | bytes 4587544
  41.3 11.1 %shard_map.145 = (bf16[640,3584]{1,0:T(8,128)(2,1)}, f32[640,3584]{1,0:T(8,128)}, f32[640,3584]{1,0:T(8,128)}, f32[1,1]{1,0:T(1,128)}, f32[256,1792]{1,0:T(8,128)S(1)}) custom-call(bf16[640,512]{1,0:T(8,128)(2,1)S(1)} %get-tuple-element.84.refs_0_, s32[512,1]{1,0:T(8,128)S(1)} %copy.23.refs_1_, s32[1,3584]{1,0:T(1,128)S(1)} %get-tuple-element.93.refs_2_, ...), custom_call_target="tpu_custom_call" | custom-call | flops 1761607680 | bytes 22937600 | tf_op jit(solution)/shard_map/pallas_call | solution.py:112
  52.4 0.8 add_reduce_fusion.2
  53.3 2.0 %fusion.3 = f16[256,1792]{1,0:T(8,128)(2,1)} fusion(bf16[640,3584]{1,0:T(8,128)(2,1)S(1)} %bitcast.13, s32[1792]{0:T(1024)S(1)} %get-tuple-element.59, f32[256]{0:T(256)S(1)} %add_reduce_fusion.2, s32[256]{0:T(256)S(1)} %get-tuple-element.57, bf16[512,640]{1,0:T(8,128)(2,1)S(1)} %copy-done.3), kind=kOutput, calls=%fused_computation.24 | convolution fusion | flops 593166336 | bytes 3549184 | tf_op jit(solution)/shard_map/dot_general | solution.py:250
  55.3 1.5 %collective-permute-start.16 = (f16[256,1792]{1,0:T(8,128)(2,1)}, f16[256,1792]{1,0:T(8,128)(2,1)S(1)}, u32[]{:S(2)}, u32[]{:S(2)}) collective-permute-start(f16[256,1792]{1,0:T(8,128)(2,1)} %fusion.3), channel_id=1, source_target_pairs={{0,2},{1,3},{2,0},{3,1},{4,6},{5,7},{6,4},{7,5},{8,10},{9,11},{10,... | collective-permute-start | bytes 2752520 | tf_op jit(solution)/shard_map/ppermute | solution.py:198
  56.8 0.8 add_reduce_fusion.3
  57.7 0.7 slice_convert_fusion.refs_9_
  58.4 1.0 convolution_add_fusion.3
  59.4 2.8 %add_convert_fusion = (f16[128,1792]{1,0:T(8,128)(2,1)}, f32[128,1792]{1,0:T(8,128)S(1)}) fusion(f32[256,1792]{1,0:T(8,128)S(1)} %get-tuple-element.36, f16[256,1792]{1,0:T(8,128)(2,1)} %collective-permute-done.9, f32[]{:T(128)} %bitcast.4), kind=kLoop, calls=%fused_computation.108 | loop fusion | flops 1605632 | bytes 4128772 | tf_op jit(solution)/shard_map/convert_element_type | solution.py:327
  62.2 0.4 collective-permute-start.10
  62.6 3.2 %fusion.69 = (f16[128,1792]{1,0:T(8,128)(2,1)}, f32[128,1792]{1,0:T(8,128)S(1)}) fusion(f32[256,1792]{1,0:T(8,128)S(1)} %convolution_add_fusion.3, f16[256,1792]{1,0:T(8,128)(2,1)} %collective-permute-done.11, f32[]{:T(128)} %bitcast.4), kind=kLoop, calls=%fused_computation.97 | loop fusion | flops 1605632 | bytes 4128772 | tf_op jit(solution)/shard_map/convert_element_type | solution.py:327
  65.8 1.6 %collective-permute-start.15 = (f16[128,1792]{1,0:T(8,128)(2,1)}, f16[128,1792]{1,0:T(8,128)(2,1)}, u32[]{:S(2)}, u32[]{:S(2)}) collective-permute-start(f16[128,1792]{1,0:T(8,128)(2,1)} %get-tuple-element.69), channel_id=1, source_target_pairs={{0,2},{1,3},{2,0},{3,1},{4,6},{5,7},{6,4},{7,5},{8,10},{9,11},{10,... | collective-permute-start | bytes 1376264 | tf_op jit(solution)/shard_map/ppermute | solution.py:198
  67.4 9.6 %shard_map.146 = (bf16[640,3584]{1,0:T(8,128)(2,1)}, f32[640,3584]{1,0:T(8,128)}, f32[640,3584]{1,0:T(8,128)}, f32[1,1]{1,0:T(1,128)}) custom-call(bf16[640,512]{1,0:T(8,128)(2,1)S(1)} %get-tuple-element.85.refs_0_, s32[512,1]{1,0:T(8,128)S(1)} %copy.23.refs_1_, s32[1,3584]{1,0:T(1,128)S(1)} %get-tuple-element.92.refs_2_, f32[512,1]{1,0:T(8,128)S(1)} %reshape.159.refs_3_, ...), custom_call_target="tpu_custom_call" | custom-call | flops 1174405120 | bytes 22937600 | tf_op jit(solution)/shard_map/pallas_call | solution.py:112
  76.9 0.7 add_reduce_fusion.1
  77.6 1.0 convolution_add_fusion.1
  78.6 2.0 %fusion.71 = (f16[128,1792]{1,0:T(8,128)(2,1)S(1)}, f32[128,1792]{1,0:T(8,128)S(1)}) fusion(f32[256,1792]{1,0:T(8,128)S(1)} %convolution_add_fusion.1, f16[256,1792]{1,0:T(8,128)(2,1)} %collective-permute-done.13, f32[]{:T(128)} %bitcast.5), kind=kLoop, calls=%fused_computation.100 | loop fusion | flops 1605632 | bytes 4128772 | tf_op jit(solution)/shard_map/convert_element_type | solution.py:327
  80.6 0.5 collective-permute-start.14
  81.2 0.7 add_reduce_fusion
  81.9 1.0 convolution_add_fusion
  82.9 0.8 fusion.66
  83.7 1.7 %collective-permute-start.17 = (f16[128,1792]{1,0:T(8,128)(2,1)S(1)}, f16[128,1792]{1,0:T(8,128)(2,1)S(1)}, u32[]{:S(2)}, u32[]{:S(2)}) collective-permute-start(f16[128,1792]{1,0:T(8,128)(2,1)S(1)} %get-tuple-element.71), channel_id=1, source_target_pairs={{0,1},{1,0},{2,3},{3,2},{4,5},{5,4},{6,7},{7,6},{8,9},{9,8},{10,11... | collective-permute-start | bytes 1376264 | tf_op jit(solution)/shard_map/ppermute | solution.py:198
  85.4 1.8 %fusion.85 = (f16[64,1792]{1,0:T(8,128)(2,1)S(1)}, f32[64,1792]{1,0:T(8,128)S(1)}) fusion(f32[128,1792]{1,0:T(8,128)S(1)} %get-tuple-element.68.refs_7_, f16[128,1792]{1,0:T(8,128)(2,1)} %collective-permute-done.10, f32[]{:T(128)} %bitcast.5), kind=kLoop, calls=%fused_computation.127 | loop fusion | flops 802816 | bytes 2064388 | tf_op jit(solution)/shard_map/convert_element_type | solution.py:327
  87.1 2.3 %collective-permute-start.12 = (f16[64,1792]{1,0:T(8,128)(2,1)S(1)}, f16[64,1792]{1,0:T(8,128)(2,1)S(1)}, u32[]{:S(2)}, u32[]{:S(2)}) collective-permute-start(f16[64,1792]{1,0:T(8,128)(2,1)S(1)} %get-tuple-element.73), channel_id=1, source_target_pairs={{0,4},{1,5},{2,6},{3,7},{4,0},{5,1},{6,2},{7,3},{8,12},{9,13},{10,... | collective-permute-start | bytes 688136 | tf_op jit(solution)/shard_map/ppermute | solution.py:198
  89.5 1.7 %fusion.78 = (f16[64,1792]{1,0:T(8,128)(2,1)S(1)}, f32[64,1792]{1,0:T(8,128)S(1)}) fusion(f32[128,1792]{1,0:T(8,128)S(1)} %get-tuple-element.70.refs_8_, f16[128,1792]{1,0:T(8,128)(2,1)} %collective-permute-done.15, f32[]{:T(128)} %bitcast.5), kind=kLoop, calls=%fused_computation.115 | loop fusion | flops 802816 | bytes 2064388 | tf_op jit(solution)/shard_map/convert_element_type | solution.py:327
  91.2 3.2 %collective-permute-start.19 = (f16[64,1792]{1,0:T(8,128)(2,1)S(1)}, f16[64,1792]{1,0:T(8,128)(2,1)S(1)}, u32[]{:S(2)}, u32[]{:S(2)}) collective-permute-start(f16[64,1792]{1,0:T(8,128)(2,1)S(1)} %get-tuple-element.77), channel_id=1, source_target_pairs={{0,4},{1,5},{2,6},{3,7},{4,0},{5,1},{6,2},{7,3},{8,12},{9,13},{10,... | collective-permute-start | bytes 688136 | tf_op jit(solution)/shard_map/ppermute | solution.py:198
  94.4 9.6 %shard_map.147 = (bf16[640,3584]{1,0:T(8,128)(2,1)}, f32[640,3584]{1,0:T(8,128)}, f32[640,3584]{1,0:T(8,128)}, f32[1,1]{1,0:T(1,128)}) custom-call(bf16[640,512]{1,0:T(8,128)(2,1)S(1)} %get-tuple-element.84.refs_0_, s32[512,1]{1,0:T(8,128)S(1)} %copy.23.refs_1_, ...), custom_call_target="tpu_custom_call", output_to_operand_aliasing={{0}: (7, {}), {1}: (8, {}), {2}: (9, {})} | custom-call | flops 1174405120 | bytes 22937600 | tf_op jit(solution)/shard_map/pallas_call | solution.py:112
  103.9 3.0 %collective-permute-done.14 = f16[128,1792]{1,0:T(8,128)(2,1)S(1)} collective-permute-done((f16[128,1792]{1,0:T(8,128)(2,1)S(1)}, f16[128,1792]{1,0:T(8,128)(2,1)S(1)}, u32[]{:S(2)}, u32[]{:S(2)}) %collective-permute-start.14) | collective-permute-done | bytes 458784 | tf_op jit(solution)/shard_map/ppermute | solution.py:198
  106.9 0.8 fusion.80
  107.8 0.8 fusion.76
  108.6 3.0 %collective-permute-start.20 = (f16[64,1792]{1,0:T(8,128)(2,1)S(1)}, f16[64,1792]{1,0:T(8,128)(2,1)S(1)}, u32[]{:S(2)}, u32[]{:S(2)}) collective-permute-start(f16[64,1792]{1,0:T(8,128)(2,1)S(1)} %get-tuple-element.79), channel_id=1, source_target_pairs={{0,4},{1,5},{2,6},{3,7},{4,0},{5,1},{6,2},{7,3},{8,12},{9,13},{10,... | collective-permute-start | bytes 688136 | tf_op jit(solution)/shard_map/ppermute | solution.py:198
  111.6 9.5 %shard_map.148 = (bf16[640,3584]{1,0:T(8,128)(2,1)}, f32[640,3584]{1,0:T(8,128)}, f32[640,3584]{1,0:T(8,128)}, f32[1,1]{1,0:T(1,128)}) custom-call(bf16[640,512]{1,0:T(8,128)(2,1)S(1)} %get-tuple-element.85.refs_0_, s32[512,1]{1,0:T(8,128)S(1)} %copy.23.refs_1_, ...), custom_call_target="tpu_custom_call", output_to_operand_aliasing={{0}: (7, {}), {1}: (8, {}), {2}: (9, {})} | custom-call | flops 1174405120 | bytes 22937600 | tf_op jit(solution)/shard_map/pallas_call | solution.py:112
  121.1 2.7 %collective-permute-done.18 = f16[64,1792]{1,0:T(8,128)(2,1)S(1)} collective-permute-done((f16[64,1792]{1,0:T(8,128)(2,1)S(1)}, f16[64,1792]{1,0:T(8,128)(2,1)S(1)}, u32[]{:S(2)}, u32[]{:S(2)}) %collective-permute-start.18) | collective-permute-done | bytes 229408 | tf_op jit(solution)/shard_map/ppermute | solution.py:198
  123.8 0.7 add_add_fusion.3
  124.6 0.7 add_add_fusion.2
  125.3 0.7 add_add_fusion.4
  126.0 2.8 %collective-permute-done.20 = f16[64,1792]{1,0:T(8,128)(2,1)S(1)} collective-permute-done((f16[64,1792]{1,0:T(8,128)(2,1)S(1)}, f16[64,1792]{1,0:T(8,128)(2,1)S(1)}, u32[]{:S(2)}, u32[]{:S(2)}) %collective-permute-start.20) | collective-permute-done | bytes 229408 | tf_op jit(solution)/shard_map/ppermute | solution.py:198
  128.8 0.7 add_add_fusion.1
  129.5 1.0 fusion.74
  (74 shorter events, 1.6 us)
Async XLA Ops:
  0.6 11.0 %copy-start.1 = (bf16[128,640]{1,0:T(8,128)(2,1)S(1)}, bf16[128,640]{1,0:T(8,128)(2,1)}, u32[]{:S(2)}) copy-start(bf16[128,640]{1,0:T(8,128)(2,1)} %refs_0_.1) | copy-start | bytes 491524
  0.6 9.4 %copy-start.9 = (f32[16]{0:T(128)S(1)}, f32[16]{0:T(128)}, u32[]{:S(2)}) copy-start(f32[16]{0:T(128)} %param.11) | copy-start | bytes 196
  0.7 11.0 %collective-permute-start.3 = (bf16[128,640]{1,0:T(8,128)(2,1)}, bf16[128,640]{1,0:T(8,128)(2,1)S(1)}, u32[]{:S(2)}, u32[]{:S(2)}) collective-permute-start(bf16[128,640]{1,0:T(8,128)(2,1)} %refs_0_.1), channel_id=1, source_target_pairs={{0,16},{8,24},{16,0},{24,8},{1,17},{9,25},{17,1},{25,9},{2,18},{10... | collective-permute-start | bytes 491528 | tf_op jit(solution)/shard_map/ppermute | solution.py:198
  3.7 8.0 %collective-permute-start.2 = (bf16[128,640]{1,0:T(8,128)(2,1)}, bf16[128,640]{1,0:T(8,128)(2,1)S(1)}, u32[]{:S(2)}, u32[]{:S(2)}) collective-permute-start(bf16[128,640]{1,0:T(8,128)(2,1)} %refs_0_.1), channel_id=1, source_target_pairs={{0,8},{8,0},{16,24},{24,16},{1,9},{9,1},{17,25},{25,17},{2,10},{10... | collective-permute-start | bytes 491528 | tf_op jit(solution)/shard_map/ppermute | solution.py:198
  3.7 8.0 %collective-permute-start.4 = (bf16[128,640]{1,0:T(8,128)(2,1)}, bf16[128,640]{1,0:T(8,128)(2,1)S(1)}, u32[]{:S(2)}, u32[]{:S(2)}) collective-permute-start(bf16[128,640]{1,0:T(8,128)(2,1)} %refs_0_.1), channel_id=1, source_target_pairs={{0,24},{8,16},{16,8},{24,0},{1,25},{9,17},{17,9},{25,1},{2,26},{10... | collective-permute-start | bytes 491528 | tf_op jit(solution)/shard_map/ppermute | solution.py:198
  4.6 5.4 %collective-permute-start = (f32[32,16]{1,0:T(8,128)S(1)}, f32[32,16]{1,0:T(8,128)S(1)}, u32[]{:S(2)}, u32[]{:S(2)}) collective-permute-start(f32[32,16]{1,0:T(8,128)S(1)} %broadcast_select_fusion), channel_id=1, source_target_pairs={{0,1},{1,0},{2,3},{3,2},{4,5},{5,4},{6,7},{7,6},{8,9},{9,8},{10,11... | collective-permute-start | bytes 6152 | tf_op jit(solution)/shard_map/ppermute | solution.py:198
  7.4 16.2 %copy-start.6 = (s32[1792]{0:T(1024)}, s32[1792]{0:T(1024)S(1)}, u32[]{:S(2)}) copy-start(s32[1792]{0:T(1024)S(1)} %get-tuple-element.60) | copy-start | bytes 21508
  10.1 5.2 %collective-permute-start.1 = (f32[32,16]{1,0:T(8,128)S(1)}, f32[32,16]{1,0:T(8,128)S(1)}, u32[]{:S(2)}, u32[]{:S(2)}) collective-permute-start(f32[32,16]{1,0:T(8,128)S(1)} %fusion.95), channel_id=1, source_target_pairs={{0,2},{1,3},{2,0},{3,1},{4,6},{5,7},{6,4},{7,5},{8,10},{9,11},{10,... | collective-permute-start | bytes 6152 | tf_op jit(solution)/shard_map/ppermute | solution.py:198
  13.8 14.7 %copy-start.4 = (bf16[512,640]{1,0:T(8,128)(2,1)}, bf16[512,640]{1,0:T(8,128)(2,1)S(1)}, u32[]{:S(2)}) copy-start(bf16[512,640]{1,0:T(8,128)(2,1)S(1)} %get-tuple-element.34) | copy-start | bytes 1966084
  13.8 19.2 %copy-start.2 = (bf16[512,640]{1,0:T(8,128)(2,1)}, bf16[512,640]{1,0:T(8,128)(2,1)S(1)}, u32[]{:S(2)}) copy-start(bf16[512,640]{1,0:T(8,128)(2,1)S(1)} %get-tuple-element.31) | copy-start | bytes 1966084
  15.3 5.0 %collective-permute-start.5 = (f32[32,16]{1,0:T(8,128)S(1)}, f32[32,16]{1,0:T(8,128)S(1)}, u32[]{:S(2)}, u32[]{:S(2)}) collective-permute-start(f32[32,16]{1,0:T(8,128)S(1)} %add_add_fusion.6), channel_id=1, source_target_pairs={{0,4},{1,5},{2,6},{3,7},{4,0},{5,1},{6,2},{7,3},{8,12},{9,13},{10,... | collective-permute-start | bytes 6152 | tf_op jit(solution)/shard_map/ppermute | solution.py:198
  20.9 14.9 %collective-permute-start.8 = (f32[32,16]{1,0:T(8,128)S(1)}, f32[32,16]{1,0:T(8,128)S(1)}, u32[]{:S(2)}, u32[]{:S(2)}) collective-permute-start(f32[32,16]{1,0:T(8,128)S(1)} %add.608), channel_id=1, source_target_pairs={{0,24},{8,16},{16,8},{24,0},{1,25},{9,17},{17,9},{25,1},{2,26},{10... | collective-permute-start | bytes 6152 | tf_op jit(solution)/shard_map/ppermute | solution.py:198
  20.9 15.4 %collective-permute-start.7 = (f32[32,16]{1,0:T(8,128)S(1)}, f32[32,16]{1,0:T(8,128)S(1)}, u32[]{:S(2)}, u32[]{:S(2)}) collective-permute-start(f32[32,16]{1,0:T(8,128)S(1)} %add.608), channel_id=1, source_target_pairs={{0,16},{8,24},{16,0},{24,8},{1,17},{9,25},{17,1},{25,9},{2,18},{10... | collective-permute-start | bytes 6152 | tf_op jit(solution)/shard_map/ppermute | solution.py:198
  22.4 13.9 %collective-permute-start.6 = (f32[32,16]{1,0:T(8,128)S(1)}, f32[32,16]{1,0:T(8,128)S(1)}, u32[]{:S(2)}, u32[]{:S(2)}) collective-permute-start(f32[32,16]{1,0:T(8,128)S(1)} %add.608), channel_id=1, source_target_pairs={{0,8},{8,0},{16,24},{24,16},{1,9},{9,1},{17,25},{25,17},{2,10},{10... | collective-permute-start | bytes 6152 | tf_op jit(solution)/shard_map/ppermute | solution.py:198
  23.4 5.2 %slice-start = ((s8[4587520]{0:T(1024)(128)(4,1)}), s8[4194304]{0:T(1024)(128)(4,1)S(1)}, s32[]{:S(2)}) async-start(s8[4587520]{0:T(1024)(128)(4,1)} %bitcast.8), calls=%async_computation | async-start | bytes 8388608
  23.6 4.9 %slice-start.1 = ((s8[4587520]{0:T(1024)(128)(4,1)}), s8[393216]{0:T(1024)(128)(4,1)S(1)}, s32[]{:S(2)}) async-start(s8[4587520]{0:T(1024)(128)(4,1)} %bitcast.8), calls=%async_computation.1 | async-start | bytes 786432
  28.1 34.5 %collective-permute-start.11 = (f16[256,1792]{1,0:T(8,128)(2,1)}, f16[256,1792]{1,0:T(8,128)(2,1)}, u32[]{:S(2)}, u32[]{:S(2)}) collective-permute-start(f16[256,1792]{1,0:T(8,128)(2,1)} %fusion), channel_id=1, source_target_pairs={{0,1},{1,0},{2,3},{3,2},{4,5},{5,4},{6,7},{7,6},{8,9},{9,8},{10,11... | collective-permute-start | bytes 2752520 | tf_op jit(solution)/shard_map/ppermute | solution.py:198
  28.5 4.5 %copy-start.8 = (s32[1792]{0:T(1024)S(1)}, s32[1792]{0:T(1024)}, u32[]{:S(2)}) copy-start(s32[1792]{0:T(1024)} %get-tuple-element.62) | copy-start | bytes 21508
  31.3 47.3 %collective-permute-start.13 = (f16[256,1792]{1,0:T(8,128)(2,1)}, f16[256,1792]{1,0:T(8,128)(2,1)}, u32[]{:S(2)}, u32[]{:S(2)}) collective-permute-start(f16[256,1792]{1,0:T(8,128)(2,1)} %fusion.2), channel_id=1, source_target_pairs={{0,1},{1,0},{2,3},{3,2},{4,5},{5,4},{6,7},{7,6},{8,9},{9,8},{10,11... | collective-permute-start | bytes 2752520 | tf_op jit(solution)/shard_map/ppermute | solution.py:198
  33.0 20.2 %slice-start.4 = ((s8[4587520]{0:T(1024)(128)(4,1)}), s8[393216]{0:T(1024)(128)(4,1)S(1)}, s32[]{:S(2)}) async-start(s8[4587520]{0:T(1024)(128)(4,1)} %bitcast.12), calls=%async_computation.4 | async-start | bytes 786432
  35.8 23.6 %collective-permute-start.9 = (f16[256,1792]{1,0:T(8,128)(2,1)}, f16[256,1792]{1,0:T(8,128)(2,1)}, u32[]{:S(2)}, u32[]{:S(2)}) collective-permute-start(f16[256,1792]{1,0:T(8,128)(2,1)} %fusion.1), channel_id=1, source_target_pairs={{0,2},{1,3},{2,0},{3,1},{4,6},{5,7},{6,4},{7,5},{8,10},{9,11},{10,... | collective-permute-start | bytes 2752520 | tf_op jit(solution)/shard_map/ppermute | solution.py:198
  39.0 2.3 %copy-start = (bf16[640,3584]{1,0:T(8,128)(2,1)S(1)}, bf16[640,3584]{1,0:T(8,128)(2,1)}, u32[]{:S(2)}) copy-start(bf16[640,3584]{1,0:T(8,128)(2,1)} %refs_4_.6) | copy-start | bytes 13762564
  41.3 11.9 %slice-start.5 = ((s8[4587520]{0:T(1024)(128)(4,1)}), s8[4194304]{0:T(1024)(128)(4,1)S(1)}, s32[]{:S(2)}) async-start(s8[4587520]{0:T(1024)(128)(4,1)} %bitcast.12), calls=%async_computation.5 | async-start | bytes 8388608
  41.3 11.9 %copy-start.3 = (bf16[512,640]{1,0:T(8,128)(2,1)S(1)}, bf16[512,640]{1,0:T(8,128)(2,1)}, u32[]{:S(2)}) copy-start(bf16[512,640]{1,0:T(8,128)(2,1)} %copy-done.2) | copy-start | bytes 1966084
  53.3 5.1 %copy-start.5 = (bf16[512,640]{1,0:T(8,128)(2,1)S(1)}, bf16[512,640]{1,0:T(8,128)(2,1)}, u32[]{:S(2)}) copy-start(bf16[512,640]{1,0:T(8,128)(2,1)} %copy-done.4) | copy-start | bytes 1966084
  53.3 5.1 %copy-start.7 = (s32[1792]{0:T(1024)S(1)}, s32[1792]{0:T(1024)}, u32[]{:S(2)}) copy-start(s32[1792]{0:T(1024)} %copy-done.6) | copy-start | bytes 21508
  55.3 27.6 %collective-permute-start.16 = (f16[256,1792]{1,0:T(8,128)(2,1)}, f16[256,1792]{1,0:T(8,128)(2,1)S(1)}, u32[]{:S(2)}, u32[]{:S(2)}) collective-permute-start(f16[256,1792]{1,0:T(8,128)(2,1)} %fusion.3), channel_id=1, source_target_pairs={{0,2},{1,3},{2,0},{3,1},{4,6},{5,7},{6,4},{7,5},{8,10},{9,11},{10,... | collective-permute-start | bytes 2752520 | tf_op jit(solution)/shard_map/ppermute | solution.py:198
  62.2 23.2 %collective-permute-start.10 = (f16[128,1792]{1,0:T(8,128)(2,1)}, f16[128,1792]{1,0:T(8,128)(2,1)}, u32[]{:S(2)}, u32[]{:S(2)}) collective-permute-start(f16[128,1792]{1,0:T(8,128)(2,1)} %get-tuple-element.67), channel_id=1, source_target_pairs={{0,1},{1,0},{2,3},{3,2},{4,5},{5,4},{6,7},{7,6},{8,9},{9,8},{10,11... | collective-permute-start | bytes 1376264 | tf_op jit(solution)/shard_map/ppermute | solution.py:198
  62.6 15.0 %slice-start.2 = ((s8[4587520]{0:T(1024)(128)(4,1)}), s8[4194304]{0:T(1024)(128)(4,1)S(1)}, s32[]{:S(2)}) async-start(s8[4587520]{0:T(1024)(128)(4,1)} %bitcast.10), calls=%async_computation.2 | async-start | bytes 8388608
  65.8 23.7 %collective-permute-start.15 = (f16[128,1792]{1,0:T(8,128)(2,1)}, f16[128,1792]{1,0:T(8,128)(2,1)}, u32[]{:S(2)}, u32[]{:S(2)}) collective-permute-start(f16[128,1792]{1,0:T(8,128)(2,1)} %get-tuple-element.69), channel_id=1, source_target_pairs={{0,2},{1,3},{2,0},{3,1},{4,6},{5,7},{6,4},{7,5},{8,10},{9,11},{10,... | collective-permute-start | bytes 1376264 | tf_op jit(solution)/shard_map/ppermute | solution.py:198
  67.3 10.2 %slice-start.3 = ((s8[4587520]{0:T(1024)(128)(4,1)}), s8[393216]{0:T(1024)(128)(4,1)S(1)}, s32[]{:S(2)}) async-start(s8[4587520]{0:T(1024)(128)(4,1)} %bitcast.10), calls=%async_computation.3 | async-start | bytes 786432
  80.6 26.3 %collective-permute-start.14 = (f16[128,1792]{1,0:T(8,128)(2,1)S(1)}, f16[128,1792]{1,0:T(8,128)(2,1)S(1)}, u32[]{:S(2)}, u32[]{:S(2)}) collective-permute-start(f16[128,1792]{1,0:T(8,128)(2,1)S(1)} %get-tuple-element.65), channel_id=1, source_target_pairs={{0,2},{1,3},{2,0},{3,1},{4,6},{5,7},{6,4},{7,5},{8,10},{9,11},{10,... | collective-permute-start | bytes 1376264 | tf_op jit(solution)/shard_map/ppermute | solution.py:198
  83.7 24.1 %collective-permute-start.17 = (f16[128,1792]{1,0:T(8,128)(2,1)S(1)}, f16[128,1792]{1,0:T(8,128)(2,1)S(1)}, u32[]{:S(2)}, u32[]{:S(2)}) collective-permute-start(f16[128,1792]{1,0:T(8,128)(2,1)S(1)} %get-tuple-element.71), channel_id=1, source_target_pairs={{0,1},{1,0},{2,3},{3,2},{4,5},{5,4},{6,7},{7,6},{8,9},{9,8},{10,11... | collective-permute-start | bytes 1376264 | tf_op jit(solution)/shard_map/ppermute | solution.py:198
  87.1 38.2 %collective-permute-start.12 = (f16[64,1792]{1,0:T(8,128)(2,1)S(1)}, f16[64,1792]{1,0:T(8,128)(2,1)S(1)}, u32[]{:S(2)}, u32[]{:S(2)}) collective-permute-start(f16[64,1792]{1,0:T(8,128)(2,1)S(1)} %get-tuple-element.73), channel_id=1, source_target_pairs={{0,4},{1,5},{2,6},{3,7},{4,0},{5,1},{6,2},{7,3},{8,12},{9,13},{10,... | collective-permute-start | bytes 688136 | tf_op jit(solution)/shard_map/ppermute | solution.py:198
  91.2 33.4 %collective-permute-start.19 = (f16[64,1792]{1,0:T(8,128)(2,1)S(1)}, f16[64,1792]{1,0:T(8,128)(2,1)S(1)}, u32[]{:S(2)}, u32[]{:S(2)}) collective-permute-start(f16[64,1792]{1,0:T(8,128)(2,1)S(1)} %get-tuple-element.77), channel_id=1, source_target_pairs={{0,4},{1,5},{2,6},{3,7},{4,0},{5,1},{6,2},{7,3},{8,12},{9,13},{10,... | collective-permute-start | bytes 688136 | tf_op jit(solution)/shard_map/ppermute | solution.py:198
  107.7 16.1 %collective-permute-start.18 = (f16[64,1792]{1,0:T(8,128)(2,1)S(1)}, f16[64,1792]{1,0:T(8,128)(2,1)S(1)}, u32[]{:S(2)}, u32[]{:S(2)}) collective-permute-start(f16[64,1792]{1,0:T(8,128)(2,1)S(1)} %get-tuple-element.75), channel_id=1, source_target_pairs={{0,4},{1,5},{2,6},{3,7},{4,0},{5,1},{6,2},{7,3},{8,12},{9,13},{10,... | collective-permute-start | bytes 688136 | tf_op jit(solution)/shard_map/ppermute | solution.py:198
  108.6 20.2 %collective-permute-start.20 = (f16[64,1792]{1,0:T(8,128)(2,1)S(1)}, f16[64,1792]{1,0:T(8,128)(2,1)S(1)}, u32[]{:S(2)}, u32[]{:S(2)}) collective-permute-start(f16[64,1792]{1,0:T(8,128)(2,1)S(1)} %get-tuple-element.79), channel_id=1, source_target_pairs={{0,4},{1,5},{2,6},{3,7},{4,0},{5,1},{6,2},{7,3},{8,12},{9,13},{10,... | collective-permute-start | bytes 688136 | tf_op jit(solution)/shard_map/ppermute | solution.py:198

commit v3 on v2

v3 whole, which is shorter than its diff:
```python
import functools

import jax
import jax.numpy as jnp
from jax import lax
from jax.experimental import pallas as pl
from jax.experimental.pallas import tpu as pltpu
from jax.sharding import PartitionSpec as P

noise_scale = 0.01
learn_rate = 0.002
beta_first = 0.9
beta_second = 0.99
adam_floor = 1e-08
stat_epsilon = 1e-06

f32 = jnp.float32
bf16 = jnp.bfloat16
wire = jnp.float16


def mixed_levels(mixed):
    mixed = jnp.bitwise_xor(mixed, jnp.right_shift(mixed, 15))
    mixed = mixed * 73244475
    mixed = jnp.bitwise_xor(mixed, jnp.right_shift(mixed, 13))
    level = jnp.bitwise_and(mixed, 255)
    return level.astype(f32) * (2.0 / 256.0) - 255.0 / 256.0


def member_part(seeds):
    return seeds * 1103515245


def column_part(columns, salt):
    return columns * 40503 + salt * 7919


def factor_levels(seed, column, salt):
    return mixed_levels(member_part(seed) + column_part(column, salt))


def factor_block(seeds, start, count, salt):
    columns = jnp.arange(count, dtype=jnp.int32) + start
    return factor_levels(seeds[:, None], columns[None, :], salt)


def factor_block_turned(seeds, start, count, salt):
    columns = jnp.arange(count, dtype=jnp.int32) + start
    return factor_levels(seeds[None, :], columns[:, None], salt).astype(bf16)


def adam_kernel(scale, row_tile, extra, *refs):
    left, member, unit, fitness, weight, first, second = refs[:7]
    weight_new, first_new, second_new, tick = refs[7 + extra :]
    tick[...] = jnp.zeros_like(tick)
    members = fitness.shape[0]
    center = jnp.sum(fitness[...], axis=0, keepdims=True) / members
    apart = fitness[...] - center
    spread = jnp.sum(apart * apart, axis=0, keepdims=True) / members
    scaled = apart / jnp.sqrt(spread + stat_epsilon)
    weighted = (scaled * mixed_levels(member[...] + unit[...])).astype(bf16)
    for start in range(0, left.shape[0], row_tile):
        rows = slice(start, start + row_tile)
        g = jnp.dot(left[rows, :], weighted, preferred_element_type=f32)
        f = beta_first * first[rows, :] + ((1.0 - beta_first) * scale) * g
        s = beta_second * second[rows, :] + ((1.0 - beta_second) * scale * scale) * g * g
        first_new[rows, :] = f
        second_new[rows, :] = s
        floor = s * lax.rsqrt(s) + adam_floor
        inverse = pl.reciprocal(floor, approx=True)
        inverse = inverse * (2.0 - floor * inverse)
        moved = weight[rows, :].astype(f32) + (learn_rate * f) * inverse
        weight_new[rows, :] = moved.astype(bf16)


def adam_part(left, member, unit, fitness, weight, first, second, before, wait_for, start, size):
    width, units = weight.shape
    members = member.shape[0]
    tile = max(t for t in range(128, 1281, 128) if size % t == 0 and start % t == 0)
    base = start // tile
    full = lambda dtype: jax.ShapeDtypeStruct((width, units), dtype)
    big = lambda: pl.BlockSpec((width, tile), lambda j: (0, base + j))
    fixed = lambda x: pl.BlockSpec(x.shape, lambda j: (0, 0))
    in_specs = [
        fixed(left),
        fixed(member),
        pl.BlockSpec((1, tile), lambda j: (0, base + j)),
        fixed(fitness),
        big(),
        big(),
        big(),
    ]
    args = [left, member, unit, fitness, weight, first, second]
    out_specs = [big(), big(), big(), pl.BlockSpec((1, 1), lambda j: (0, 0))]
    out_shape = [full(bf16), full(f32), full(f32), jax.ShapeDtypeStruct((1, 1), f32)]
    aliases = {}
    if before is not None:
        aliases = {len(args) + i: i for i in range(len(before))}
        args += list(before)
    args += list(wait_for)
    extra = len(args) - len(in_specs)
    in_specs += [pl.BlockSpec(memory_space=pl.ANY)] * extra
    return pl.pallas_call(
        functools.partial(adam_kernel, 1.0 / (members * noise_scale), width // 2, extra),
        grid=(size // tile,),
        in_specs=in_specs,
        out_specs=out_specs,
        out_shape=out_shape,
        input_output_aliases=aliases,
        compiler_params=pltpu.CompilerParams(vmem_limit_bytes=44 * 1024 * 1024),
        cost_estimate=pl.CostEstimate(
            flops=2 * width * size * members,
            bytes_accessed=20 * width * size,
            transcendentals=0,
        ),
    )(*args)


def sort_kernel(orders, share, index, seeds, columns, *refs):
    kinds = len(orders)
    pieces = refs[: -3 * kinds - 2]
    turned, alongs, ids = (refs[len(pieces) + i * kinds :][:kinds] for i in range(3))
    held = refs[-1]
    refs[-2][...] = jnp.zeros_like(refs[-2])
    per_piece = pieces[0].shape[0] // share
    for p, piece in enumerate(pieces):
        for k in range(per_piece):
            held[p * per_piece + k] = piece[k * share : (k + 1) * share, :]
    for mask in range(held.shape[0]):
        rows = held[index[0, mask]]
        block = pl.multiple_of(index[1, mask] * share, share)
        member = member_part(seeds[pl.ds(block, share), :])
        wide = rows.astype(f32)
        along = [
            noise_scale
            * jnp.sum(wide * mixed_levels(member + columns[i : i + 1, :]), axis=1, keepdims=True)
            for i in range(2)
        ]
        for kind, order in enumerate(orders):
            at = order.index(mask) * share
            turned[kind][at : at + share, :] = rows
            ids[kind][at : at + share, :] = member
            for i in range(2):
                alongs[kind][at : at + share, i : i + 1] = along[i]


def sort_blocks(pieces, index, seeds, columns, orders):
    members = seeds.shape[0]
    width = pieces[0].shape[1]
    shares = len(orders[0])
    share = members // shares
    kinds = len(orders)
    whole = pl.BlockSpec(memory_space=pltpu.VMEM)
    outs = pl.pallas_call(
        functools.partial(sort_kernel, orders, share),
        in_specs=[pl.BlockSpec(memory_space=pltpu.SMEM)] + [whole] * (2 + len(pieces)),
        out_specs=[whole] * (3 * kinds + 1),
        out_shape=[jax.ShapeDtypeStruct((members, width), bf16)] * kinds
        + [jax.ShapeDtypeStruct((members, 2), f32)] * kinds
        + [jax.ShapeDtypeStruct((members, 1), jnp.int32)] * kinds
        + [jax.ShapeDtypeStruct((1, 1), f32)],
        scratch_shapes=[pltpu.VMEM((shares, share, width), bf16)],
        compiler_params=pltpu.CompilerParams(vmem_limit_bytes=32 * 1024 * 1024),
    )(index, seeds[:, None], columns, *pieces)
    return outs[:kinds], outs[kinds : 2 * kinds], outs[2 * kinds : 3 * kinds], outs[-1]


def block_order(bits):
    order = [0]
    for bit in reversed(bits):
        order = order + [mask ^ (1 << bit) for mask in order]
    return order


def shards(
    tokens, seeds, fitness, gate_weight, up_weight, gate_first, up_first, gate_second, up_second
):
    members = seeds.shape[0]
    width_part, unit_part = gate_weight.shape
    shares = lax.axis_size("fsdp")
    share = members // shares
    me = lax.axis_index("fsdp")
    width_start = me * width_part
    unit_start = lax.axis_index("pop") * unit_part
    levels = shares.bit_length() - 1
    across = list(range(levels))
    along_first = [1, 0] + across[2:] if levels > 1 else across

    def exchange(x, mask, axis="fsdp"):
        size = lax.axis_size(axis)
        return lax.ppermute(x, axis, [(i, i ^ mask) for i in range(size)])

    pops = lax.axis_size("pop")
    pop = lax.axis_index("pop")
    per_pop = shares // pops
    pieces = [tokens]
    for mask in reversed(range(1, pops)):
        pieces.insert(1, exchange(tokens, mask, "pop"))

    group = members // fitness.shape[0]
    own = jnp.arange(group)[:, None] == pop * shares + me
    fit = jnp.where(own, fitness[None, :], 0.0)
    turned_gate = factor_block_turned(seeds, width_start, width_part, 1)
    fit = fit + exchange(fit, 1)
    turned_up = factor_block_turned(seeds, width_start, width_part, 3)
    fit = sum([exchange(fit, mask) for mask in range(2, shares, 2)], fit)

    masks = jnp.arange(shares)
    blocks = jnp.bitwise_xor(me, masks)
    slots = jnp.bitwise_xor(blocks // per_pop, pop) * per_pop + blocks % per_pop
    features = jnp.arange(width_part, dtype=jnp.int32) + width_start
    orders = [block_order(across), block_order(along_first)]
    bits_of = [across, along_first]
    tokens_of, along_of, member_of, tick = sort_blocks(
        pieces,
        jnp.stack([slots, blocks]).astype(jnp.int32),
        seeds,
        jnp.stack([column_part(features, 1), column_part(features, 3)]),
        orders,
    )

    columns = jnp.arange(unit_part, dtype=jnp.int32) + unit_start
    member = member_part(seeds)[:, None]

    kept_rows = slice(0, members // 2)
    sent_rows = slice(members // 2, members)
    unit_tiles = unit_part // 128
    cut = unit_tiles // 2 * 128
    plan = [("gate", 0, 1), ("up", 0, 0), ("gate", 1, 0), ("up", 1, 1)]

    def span(index):
        return (0, cut) if plan[index][1] == 0 else (cut, unit_part)

    state = {
        "gate": (turned_gate, column_part(columns, 2)[None, :], gate_weight, gate_first, gate_second),
        "up": (turned_up, column_part(columns, 4)[None, :], up_weight, up_first, up_second),
    }

    def product(index, rows, tick):
        name, _, kind = plan[index]
        start, stop = span(index)
        total = jnp.dot(
            tokens_of[kind][rows], state[name][2][:, start:stop], preferred_element_type=f32
        )
        along = along_of[kind][rows, {"gate": 0, "up": 1}[name]][:, None]
        unit = state[name][1][:, start:stop]
        return total + along * mixed_levels(member_of[kind][rows] + unit) + tick

    sent = [None] * len(plan)

    def zero_of(x):
        return x[:1, :1] * 0.0

    def send(index, tick):
        partial = product(index, sent_rows, tick).astype(wire)
        sent[index] = exchange(partial, 1 << bits_of[plan[index][2]][0])
        return partial

    fit = fit + tick
    fit = sum([exchange(fit, mask, "pop") for mask in range(1, pops)], fit).reshape(members, 1)
    wait = [send(index, tick)[:8, :128].astype(f32) for index in (0, 1)]

    updated = {"gate": None, "up": None}
    running = {}

    def update(index, wait_for=()):
        name = plan[index][0]
        left, unit, weight, first, second = state[name]
        start, stop = span(index)
        *updated[name], tick = adam_part(
            left, member, unit, fit, weight, first, second, updated[name], wait_for, start, stop - start
        )
        return tick

    def reduce_step(index, level, tick):
        if level == 0:
            running[index] = [product(index, kept_rows, tick), sent[index]]
        kept, arrived = running[index]
        rows = arrived.shape[0] // 2

        def added(part):
            part = slice(part * rows, (part + 1) * rows)
            return kept[part] + arrived[part].astype(f32) + tick

        outgoing = added(1).astype(wire)
        bit = bits_of[plan[index][2]][level + 1]
        running[index] = [added(0), exchange(outgoing, 1 << bit)]
        return running[index][0]

    def total(index, tick):
        kept, arrived = running[index]
        return kept + arrived.astype(f32) + tick

    tick = update(0, wait)
    wait = [reduce_step(index, 0, tick) for index in (1, 0)]
    wait.append(send(2, tick)[:8, :128].astype(f32))
    wait.append(send(3, zero_of(wait[0]))[:8, :128].astype(f32))
    tick = update(1, wait)
    wait = [reduce_step(index, 1, tick) for index in (1, 0)]
    wait += [reduce_step(index, 0, zero_of(wait[0])) for index in (2, 3)]
    tick = update(2, wait)
    wait = [reduce_step(index, 1, tick) for index in (2, 3)]
    tick = update(3, wait)
    for level in range(2, levels - 1):
        for index in range(len(plan)):
            reduce_step(index, level, tick)
    hidden = [
        (jax.nn.silu(total(index, tick)) * total(index + 1, tick)).astype(bf16) for index in (0, 2)
    ]
    hidden = jnp.concatenate(hidden, axis=1)
    gate_new, gate_first_new, gate_second_new = updated["gate"]
    up_new, up_first_new, up_second_new = updated["up"]
    return (hidden, gate_new, up_new, gate_first_new, up_first_new, gate_second_new, up_second_new)


def solution(mesh):
    placed = (P("pop", "fsdp"), P(), P(("pop", "fsdp"))) + (P("fsdp", "pop"),) * 6
    return jax.shard_map(
        shards,
        mesh=mesh,
        in_specs=placed,
        out_specs=(P("fsdp", "pop"),) * 7,
        check_vma=False,
    )
```

time: 132 us -> 131 us (level); the launches traced: 131 us -> 131 us
  other arithmetic: 27.7 us -> 16.7 us
  waiting for transfers between devices: 10.8 us -> 18.8 us
  matrix products: 12.9 us -> 18 us
  between operations: 3.72 us -> 2.3 us
    ppermute x21 -> x22, waiting for transfers between devices: 10.8 us -> 18.8 us  [exchange(): return lax.ppermute(x, axis, [(i, i ^ mask) for i in range(size)])]
    add x12 -> x2, other arithmetic: 6.32 us -> 0.73 us  [the longest x1 0.72 us: shards(): fit = fit + tick]
    convert_element_type x13 -> x14, other arithmetic: 17.6 us -> 12 us  [the longest x8 7.62 us: reduce_step(): outgoing = added(1).astype(wire)]
    dot_general x7 -> x8, matrix products: 12.9 us -> 18 us  [product(): jnp.dot(tokens_of[kind][rows], state[name][2][:, start:stop], preferred_e...]
    ppermute x21 -> x22, starting transfers between devices: 28 us -> 28 us  [exchange(): return lax.ppermute(x, axis, [(i, i ^ mask) for i in range(size)])]
  transfers between devices with their start and end apart: 21 -> 22, of which waited for: 4 -> 6; matrix products, arithmetic and copies ran while one was open for 32% -> 27% of each run, Pallas kernels for 32% -> 32%
where the time goes in v3:
time: 131 us
  Pallas kernels  41.6 us (32%)
  starting transfers between devices  28 us (21%)
  waiting for transfers between devices  18.8 us (14%)
  matrix products  18 us (14%)
  other arithmetic  16.7 us (13%)
  local copies, waits for them, and re-layouts  5.54 us (4%)
  between operations  2.3 us (2%)
    pallas_call x4, Pallas kernels, adam_part(): pl.pallas_call(functools.partial(adam_kernel, 1.0 / (members * noise_scal...  39 us
    ppermute x22, starting transfers between devices, exchange(): return lax.ppermute(x, axis, [(i, i ^ mask) for i in range(size)])  28 us
    ppermute x22, waiting for transfers between devices, exchange(): return lax.ppermute(x, axis, [(i, i ^ mask) for i in range(size)])  18.8 us
    dot_general x8, matrix products, product(): jnp.dot(tokens_of[kind][rows], state[name][2][:, start:stop], preferred_e...  18 us
    convert_element_type x8, other arithmetic, reduce_step(): outgoing = added(1).astype(wire)  7.62 us
  transfers between devices with their start and end apart: 22, of which 6 were waited for; matrix products, arithmetic and copies ran while one was open for 27% of the time, Pallas kernels for 32%

profile of v3, /device:TPU:0, one launch (start us, length us, event | category | flops | bytes accessed | tf_op | source)
XLA Modules:
  0.0 130.9 jit_solution(4028479411661925235)
XLA Ops:
  0.7 3.0 %collective-permute-start.1 = (bf16[128,640]{1,0:T(8,128)(2,1)}, bf16[128,640]{1,0:T(8,128)(2,1)S(1)}, u32[]{:S(2)}, u32[]{:S(2)}) collective-permute-start(bf16[128,640]{1,0:T(8,128)(2,1)} %refs_0_.1), channel_id=1, source_target_pairs={{0,16},{8,24},{16,0},{24,8},{1,17},{9,25},{17,1},{25,9},{2,18},{10... | collective-permute-start | bytes 491528 | tf_op jit(solution)/shard_map/ppermute | solution.py:191
  3.9 0.7 broadcast_select_fusion
  4.6 2.0 %collective-permute-start.3 = (f32[32,16]{1,0:T(8,128)S(1)}, f32[32,16]{1,0:T(8,128)S(1)}, u32[]{:S(2)}, u32[]{:S(2)}) collective-permute-start(f32[32,16]{1,0:T(8,128)S(1)} %broadcast_select_fusion), channel_id=1, source_target_pairs={{0,1},{1,0},{2,3},{3,2},{4,5},{5,4},{6,7},{7,6},{8,9},{9,8},{10,11... | collective-permute-start | bytes 6152 | tf_op jit(solution)/shard_map/ppermute | solution.py:191
  6.6 0.7 broadcast_multiply_fusion
  7.4 1.0 fusion.79
  8.4 0.7 fusion.114
  9.1 3.0 %collective-permute-start.5 = (f32[32,16]{1,0:T(8,128)S(1)}, f32[32,16]{1,0:T(8,128)S(1)}, u32[]{:S(2)}, u32[]{:S(2)}) collective-permute-start(f32[32,16]{1,0:T(8,128)S(1)} %fusion.114), channel_id=1, source_target_pairs={{0,4},{1,5},{2,6},{3,7},{4,0},{5,1},{6,2},{7,3},{8,12},{9,13},{10,... | collective-permute-start | bytes 6152 | tf_op jit(solution)/shard_map/ppermute | solution.py:191
  12.1 1.3 %collective-permute-start.6 = (f32[32,16]{1,0:T(8,128)S(1)}, f32[32,16]{1,0:T(8,128)S(1)}, u32[]{:S(2)}, u32[]{:S(2)}) collective-permute-start(f32[32,16]{1,0:T(8,128)S(1)} %fusion.114), channel_id=1, source_target_pairs={{0,6},{1,7},{2,4},{3,5},{4,2},{5,3},{6,0},{7,1},{8,14},{9,15},{10,... | collective-permute-start | bytes 6152 | tf_op jit(solution)/shard_map/ppermute | solution.py:191
  13.5 0.2 collective-permute-start.4
  13.8 0.8 copy.22.seeds
  14.7 2.5 %shard_map.144 = (bf16[512,640]{1,0:T(8,128)(2,1)S(1)}, bf16[512,640]{1,0:T(8,128)(2,1)S(1)}, f32[512,2]{1,0:T(8,128)S(1)}, f32[512,2]{1,0:T(8,128)S(1)}, s32[51...) custom-call(s32[2,8]{1,0:T(2,128)S(1)} %pad_add_fusion.1.index, s32[512,1]{1,0:T(8,128)S(1)} %copy.22.seeds, ...), custom_call_target="tpu_custom_call" | custom-call | tf_op jit(solution)/shard_map/pallas_call | solution.py:154
  17.3 0.4 collective-permute-done.6
  17.6 0.7 add_add_fusion.1
  18.4 1.6 %collective-permute-start.8 = (f32[32,16]{1,0:T(8,128)S(1)}, f32[32,16]{1,0:T(8,128)S(1)}, u32[]{:S(2)}, u32[]{:S(2)}) collective-permute-start(f32[32,16]{1,0:T(8,128)S(1)} %add_add_fusion.1), channel_id=1, source_target_pairs={{0,16},{8,24},{16,0},{24,8},{1,17},{9,25},{17,1},{25,9},{2,18},{10... | collective-permute-start | bytes 6152 | tf_op jit(solution)/shard_map/ppermute | solution.py:191
  19.9 0.3 collective-permute-start.7
  20.4 0.3 slice_reduce_fusion.1
  20.7 4.8 %fusion.9 = f16[256,1792]{1,0:T(8,128)(2,1)} fusion(bf16[640,3584]{1,0:T(8,128)(2,1)} %refs_4_.7, s32[1792]{0:T(1024)S(1)} %get-tuple-element.66, s32[256]{0:T(256)S(1)} %get-tuple-element.63, f32[256]{0:T(256)S(1)} %get-tuple-element.56, f32[]{:T(128)} %bitcast.2, bf16[512,640]{1,0:T(8,128)(2,1)S(1)} %get-tuple-element.34), kind=kOutput, calls=%fused_computation.33 | convolution fusion | flops 593625088 | bytes 3549696 | tf_op jit(solution)/shard_map/dot_general | solution.py:242
  25.5 0.7 slice_convert_fusion.2.refs_8_
  26.2 1.5 %collective-permute-start.12 = (f16[256,1792]{1,0:T(8,128)(2,1)}, f16[256,1792]{1,0:T(8,128)(2,1)}, u32[]{:S(2)}, u32[]{:S(2)}) collective-permute-start(f16[256,1792]{1,0:T(8,128)(2,1)} %fusion.9), channel_id=1, source_target_pairs={{0,1},{1,0},{2,3},{3,2},{4,5},{5,4},{6,7},{7,6},{8,9},{9,8},{10,11... | collective-permute-start | bytes 2752520 | tf_op jit(solution)/shard_map/ppermute | solution.py:191
  27.7 0.3 slice_reduce_fusion.2
  28.2 2.8 %fusion.8 = f16[256,1792]{1,0:T(8,128)(2,1)} fusion(bf16[640,3584]{1,0:T(8,128)(2,1)S(1)} %bitcast.12, f32[]{:T(128)} %bitcast.2, s32[256]{0:T(256)S(1)} %get-tuple-element.62, f32[256]{0:T(256)S(1)} %get-tuple-element.59, s32[1792]{0:T(1024)S(1)} %get-tuple-element.68, bf16[512,640]{1,0:T(8,128)(2,1)S(1)} %get-tuple-element.30), kind=kOutput, calls=%fused_computation.32 | convolution fusion | flops 593625088 | bytes 3549188 | tf_op jit(solution)/shard_map/dot_general | solution.py:242
  31.0 0.7 slice_convert_fusion.3.refs_7_
  31.7 1.5 %collective-permute-start.10 = (f16[256,1792]{1,0:T(8,128)(2,1)}, f16[256,1792]{1,0:T(8,128)(2,1)}, u32[]{:S(2)}, u32[]{:S(2)}) collective-permute-start(f16[256,1792]{1,0:T(8,128)(2,1)} %fusion.8), channel_id=1, source_target_pairs={{0,2},{1,3},{2,0},{3,1},{4,6},{5,7},{6,4},{7,5},{8,10},{9,11},{10,... | collective-permute-start | bytes 2752520 | tf_op jit(solution)/shard_map/ppermute | solution.py:191
  33.4 2.3 %copy-done = bf16[640,3584]{1,0:T(8,128)(2,1)S(1)} copy-done((bf16[640,3584]{1,0:T(8,128)(2,1)S(1)}, bf16[640,3584]{1,0:T(8,128)(2,1)}, u32[]{:S(2)}) %copy-start) | copy-done | bytes 4587544
  35.7 10.0 %shard_map.145 = (bf16[640,3584]{1,0:T(8,128)(2,1)}, f32[640,3584]{1,0:T(8,128)}, f32[640,3584]{1,0:T(8,128)}, f32[1,1]{1,0:T(1,128)}) custom-call(bf16[640,512]{1,0:T(8,128)(2,1)S(1)} %get-tuple-element.86.refs_0_, s32[512,1]{1,0:T(8,128)S(1)} %copy.23.refs_1_, s32[1,3584]{1,0:T(1,128)S(1)} %get-tuple-element.94.refs_2_, f32[512,1]{1,0:T(8,128)S(1)} %reshape.153.refs_3_, ...), custom_call_target="tpu_custom_call" | custom-call | flops 1174405120 | bytes 22937600 | tf_op jit(solution)/shard_map/pallas_call | solution.py:103
  45.7 2.7 %fusion.10 = f16[256,1792]{1,0:T(8,128)(2,1)} fusion(bf16[640,3584]{1,0:T(8,128)(2,1)S(1)} %copy-done, s32[1792]{0:T(1024)S(1)} %get-tuple-element.67, f32[256]{0:T(256)S(1)} %get-tuple-element.54, f32[]{:T(128)} %bitcast.3, s32[256]{0:T(256)S(1)} %get-tuple-element.63, bf16[512,640]{1,0:T(8,128)(2,1)S(1)} %copy-done.3), kind=kOutput, calls=%fused_computation.34 | convolution fusion | flops 593625088 | bytes 3549188 | tf_op jit(solution)/shard_map/dot_general | solution.py:242
  48.4 0.7 slice_convert_fusion.1.refs_9_
  49.1 0.5 collective-permute-start.15
  49.6 1.7 %fusion.4 = f32[256,1792]{1,0:T(8,128)S(1)} fusion(bf16[640,3584]{1,0:T(8,128)(2,1)S(1)} %bitcast.10, s32[256]{0:T(256)S(1)} %get-tuple-element.64, f32[256]{0:T(256)S(1)} %get-tuple-element.55, f32[]{:T(128)} %bitcast.3, s32[1792]{0:T(1024)S(1)} %get-tuple-element.66, bf16[512,640]{1,0:T(8,128)(2,1)S(1)} %copy-done.3), kind=kOutput, calls=%fused_computation.9 | convolution fusion | flops 593166336 | bytes 4466692 | tf_op jit(solution)/shard_map/dot_general | solution.py:242
  51.3 1.7 %fusion.7 = f32[256,1792]{1,0:T(8,128)S(1)} fusion(bf16[640,3584]{1,0:T(8,128)(2,1)S(1)} %copy-done, f32[]{:T(128)} %bitcast.3, s32[1792]{0:T(1024)S(1)} %get-tuple-element.68, s32[256]{0:T(256)S(1)} %get-tuple-element.61, f32[256]{0:T(256)S(1)} %get-tuple-element.60, bf16[512,640]{1,0:T(8,128)(2,1)S(1)} %get-tuple-element.30), kind=kOutput, calls=%fused_computation.15 | convolution fusion | flops 593166336 | bytes 4466692 | tf_op jit(solution)/shard_map/dot_general | solution.py:242
  53.0 2.1 %fusion.87 = (f16[128,1792]{1,0:T(8,128)(2,1)S(1)}, f32[128,1792]{1,0:T(8,128)S(1)}) fusion(f32[256,1792]{1,0:T(8,128)S(1)} %fusion.4, f16[256,1792]{1,0:T(8,128)(2,1)} %collective-permute-done.12, f32[]{:T(128)} %bitcast.3), kind=kLoop, calls=%fused_computation.120 | loop fusion | flops 1605632 | bytes 4128772 | tf_op jit(solution)/shard_map/convert_element_type | solution.py:285
  55.1 0.5 slice.280
  55.6 0.6 collective-permute-start.14
  56.8 2.1 %fusion.11 = f16[256,1792]{1,0:T(8,128)(2,1)} fusion(bf16[640,3584]{1,0:T(8,128)(2,1)S(1)} %bitcast.10, f32[]{:T(128)} %bitcast.4, s32[1792]{0:T(1024)S(1)} %get-tuple-element.65, f32[256]{0:T(256)S(1)} %get-tuple-element.57, s32[256]{0:T(256)S(1)} %get-tuple-element.62, bf16[512,640]{1,0:T(8,128)(2,1)S(1)} %get-tuple-element.30), kind=kOutput, calls=%fused_computation.35 | convolution fusion | flops 593625088 | bytes 3549188 | tf_op jit(solution)/shard_map/dot_general | solution.py:242
  59.0 1.5 %collective-permute-start.17 = (f16[256,1792]{1,0:T(8,128)(2,1)}, f16[256,1792]{1,0:T(8,128)(2,1)S(1)}, u32[]{:S(2)}, u32[]{:S(2)}) collective-permute-start(f16[256,1792]{1,0:T(8,128)(2,1)} %fusion.11), channel_id=1, source_target_pairs={{0,2},{1,3},{2,0},{3,1},{4,6},{5,7},{6,4},{7,5},{8,10},{9,11},{10,... | collective-permute-start | bytes 2752520 | tf_op jit(solution)/shard_map/ppermute | solution.py:191
  60.4 2.0 %fusion.90 = (f16[128,1792]{1,0:T(8,128)(2,1)S(1)}, f32[128,1792]{1,0:T(8,128)S(1)}) fusion(f32[256,1792]{1,0:T(8,128)S(1)} %fusion.7, f16[256,1792]{1,0:T(8,128)(2,1)} %collective-permute-done.10, f32[]{:T(128)} %bitcast.3), kind=kLoop, calls=%fused_computation.125 | loop fusion | flops 1605632 | bytes 4128772 | tf_op jit(solution)/shard_map/convert_element_type | solution.py:285
  62.5 1.6 %collective-permute-start.11 = (f16[128,1792]{1,0:T(8,128)(2,1)S(1)}, f16[128,1792]{1,0:T(8,128)(2,1)S(1)}, u32[]{:S(2)}, u32[]{:S(2)}) collective-permute-start(f16[128,1792]{1,0:T(8,128)(2,1)S(1)} %get-tuple-element.71), channel_id=1, source_target_pairs={{0,1},{1,0},{2,3},{3,2},{4,5},{5,4},{6,7},{7,6},{8,9},{9,8},{10,11... | collective-permute-start | bytes 1376264 | tf_op jit(solution)/shard_map/ppermute | solution.py:191
  64.1 0.7 slice_convert_fusion.refs_10_
  64.7 9.7 %shard_map.146 = (bf16[640,3584]{1,0:T(8,128)(2,1)}, f32[640,3584]{1,0:T(8,128)}, f32[640,3584]{1,0:T(8,128)}, f32[1,1]{1,0:T(1,128)}) custom-call(bf16[640,512]{1,0:T(8,128)(2,1)S(1)} %get-tuple-element.85.refs_0_, s32[512,1]{1,0:T(8,128)S(1)} %copy.23.refs_1_, s32[1,3584]{1,0:T(1,128)S(1)} %get-tuple-element.93.refs_2_, f32[512,1]{1,0:T(8,128)S(1)} %reshape.153.refs_3_, ...), custom_call_target="tpu_custom_call" | custom-call | flops 1174405120 | bytes 22937600 | tf_op jit(solution)/shard_map/pallas_call | solution.py:103
  74.4 0.8 fusion.97
  75.2 0.6 slice.288
  76.4 4.6 %collective-permute-done.11 = f16[128,1792]{1,0:T(8,128)(2,1)S(1)} collective-permute-done((f16[128,1792]{1,0:T(8,128)(2,1)S(1)}, f16[128,1792]{1,0:T(8,128)(2,1)S(1)}, u32[]{:S(2)}, u32[]{:S(2)}) %collective-permute-start.11) | collective-permute-done | bytes 458784 | tf_op jit(solution)/shard_map/ppermute | solution.py:191
  81.0 0.8 fusion.102
  81.8 1.8 %collective-permute-start.13 = (f16[64,1792]{1,0:T(8,128)(2,1)S(1)}, f16[64,1792]{1,0:T(8,128)(2,1)S(1)}, u32[]{:S(2)}, u32[]{:S(2)}) collective-permute-start(f16[64,1792]{1,0:T(8,128)(2,1)S(1)} %get-tuple-element.77), channel_id=1, source_target_pairs={{0,4},{1,5},{2,6},{3,7},{4,0},{5,1},{6,2},{7,3},{8,12},{9,13},{10,... | collective-permute-start | bytes 688136 | tf_op jit(solution)/shard_map/ppermute | solution.py:191
  83.5 1.2 collective-permute-start.19
  84.8 1.1 fusion.1
  85.9 0.2 fusion.84
  86.1 0.6 collective-permute-start.16
  86.7 1.1 fusion
  87.8 5.1 %collective-permute-done.17 = f16[256,1792]{1,0:T(8,128)(2,1)S(1)} collective-permute-done((f16[256,1792]{1,0:T(8,128)(2,1)}, f16[256,1792]{1,0:T(8,128)(2,1)S(1)}, u32[]{:S(2)}, u32[]{:S(2)}) %collective-permute-start.17) | collective-permute-done | bytes 917536 | tf_op jit(solution)/shard_map/ppermute | solution.py:191
  92.9 0.2 fusion.81
  93.1 2.6 %collective-permute-start.18 = (f16[128,1792]{1,0:T(8,128)(2,1)S(1)}, f16[128,1792]{1,0:T(8,128)(2,1)S(1)}, u32[]{:S(2)}, u32[]{:S(2)}) collective-permute-start(f16[128,1792]{1,0:T(8,128)(2,1)S(1)} %get-tuple-element.73), channel_id=1, source_target_pairs={{0,1},{1,0},{2,3},{3,2},{4,5},{5,4},{6,7},{7,6},{8,9},{9,8},{10,11... | collective-permute-start | bytes 1376264 | tf_op jit(solution)/shard_map/ppermute | solution.py:191
  95.7 9.7 %shard_map.147 = (bf16[640,3584]{1,0:T(8,128)(2,1)}, f32[640,3584]{1,0:T(8,128)}, f32[640,3584]{1,0:T(8,128)}, f32[1,1]{1,0:T(1,128)}) custom-call(bf16[640,512]{1,0:T(8,128)(2,1)S(1)} %get-tuple-element.86.refs_0_, s32[512,1]{1,0:T(8,128)S(1)} %copy.23.refs_1_, ...), custom_call_target="tpu_custom_call", output_to_operand_aliasing={{0}: (7, {}), {1}: (8, {}), {2}: (9, {})} | custom-call | flops 1174405120 | bytes 22937600 | tf_op jit(solution)/shard_map/pallas_call | solution.py:103
  105.4 1.3 %collective-permute-done.16 = f16[128,1792]{1,0:T(8,128)(2,1)S(1)} collective-permute-done((f16[128,1792]{1,0:T(8,128)(2,1)S(1)}, f16[128,1792]{1,0:T(8,128)(2,1)S(1)}, u32[]{:S(2)}, u32[]{:S(2)}) %collective-permute-start.16) | collective-permute-done | bytes 458784 | tf_op jit(solution)/shard_map/ppermute | solution.py:191
  106.8 0.8 fusion.95
  107.5 1.8 %collective-permute-start.20 = (f16[64,1792]{1,0:T(8,128)(2,1)S(1)}, f16[64,1792]{1,0:T(8,128)(2,1)S(1)}, u32[]{:S(2)}, u32[]{:S(2)}) collective-permute-start(f16[64,1792]{1,0:T(8,128)(2,1)S(1)} %get-tuple-element.81), channel_id=1, source_target_pairs={{0,4},{1,5},{2,6},{3,7},{4,0},{5,1},{6,2},{7,3},{8,12},{9,13},{10,... | collective-permute-start | bytes 688136 | tf_op jit(solution)/shard_map/ppermute | solution.py:191
  109.3 0.8 fusion.93
  110.1 1.3 collective-permute-start.21
  111.4 9.7 %shard_map.148 = (bf16[640,3584]{1,0:T(8,128)(2,1)}, f32[640,3584]{1,0:T(8,128)}, f32[640,3584]{1,0:T(8,128)}, f32[1,1]{1,0:T(1,128)}) custom-call(bf16[640,512]{1,0:T(8,128)(2,1)S(1)} %get-tuple-element.85.refs_0_, s32[512,1]{1,0:T(8,128)S(1)} %copy.23.refs_1_, ...), custom_call_target="tpu_custom_call", output_to_operand_aliasing={{0}: (7, {}), {1}: (8, {}), {2}: (9, {})} | custom-call | flops 1174405120 | bytes 22937600 | tf_op jit(solution)/shard_map/pallas_call | solution.py:103
  121.0 0.8 multiply_convert_fusion.1
  121.9 2.5 %collective-permute-done.20 = f16[64,1792]{1,0:T(8,128)(2,1)S(1)} collective-permute-done((f16[64,1792]{1,0:T(8,128)(2,1)S(1)}, f16[64,1792]{1,0:T(8,128)(2,1)S(1)}, u32[]{:S(2)}, u32[]{:S(2)}) %collective-permute-start.20) | collective-permute-done | bytes 229408 | tf_op jit(solution)/shard_map/ppermute | solution.py:191
  124.4 4.8 %collective-permute-done.21 = f16[64,1792]{1,0:T(8,128)(2,1)S(1)} collective-permute-done((f16[64,1792]{1,0:T(8,128)(2,1)S(1)}, f16[64,1792]{1,0:T(8,128)(2,1)S(1)}, u32[]{:S(2)}, u32[]{:S(2)}) %collective-permute-start.21) | collective-permute-done | bytes 229408 | tf_op jit(solution)/shard_map/ppermute | solution.py:191
  129.2 0.8 multiply_convert_fusion
  130.1 0.8 pad_maximum_fusion
  (52 shorter events, 1.1 us)
Async XLA Ops:
  0.6 14.1 %copy-start.1 = (bf16[128,640]{1,0:T(8,128)(2,1)S(1)}, bf16[128,640]{1,0:T(8,128)(2,1)}, u32[]{:S(2)}) copy-start(bf16[128,640]{1,0:T(8,128)(2,1)} %refs_0_.1) | copy-start | bytes 491524
  0.6 17.0 %copy-start.4 = (f32[16]{0:T(128)S(1)}, f32[16]{0:T(128)}, u32[]{:S(2)}) copy-start(f32[16]{0:T(128)} %param.11) | copy-start | bytes 196
  0.7 12.8 %collective-permute-start.1 = (bf16[128,640]{1,0:T(8,128)(2,1)}, bf16[128,640]{1,0:T(8,128)(2,1)S(1)}, u32[]{:S(2)}, u32[]{:S(2)}) collective-permute-start(bf16[128,640]{1,0:T(8,128)(2,1)} %refs_0_.1), channel_id=1, source_target_pairs={{0,16},{8,24},{16,0},{24,8},{1,17},{9,25},{17,1},{25,9},{2,18},{10... | collective-permute-start | bytes 491528 | tf_op jit(solution)/shard_map/ppermute | solution.py:191
  3.7 11.0 %collective-permute-start = (bf16[128,640]{1,0:T(8,128)(2,1)}, bf16[128,640]{1,0:T(8,128)(2,1)S(1)}, u32[]{:S(2)}, u32[]{:S(2)}) collective-permute-start(bf16[128,640]{1,0:T(8,128)(2,1)} %refs_0_.1), channel_id=1, source_target_pairs={{0,8},{8,0},{16,24},{24,16},{1,9},{9,1},{17,25},{25,17},{2,10},{10... | collective-permute-start | bytes 491528 | tf_op jit(solution)/shard_map/ppermute | solution.py:191
  3.7 11.0 %collective-permute-start.2 = (bf16[128,640]{1,0:T(8,128)(2,1)}, bf16[128,640]{1,0:T(8,128)(2,1)S(1)}, u32[]{:S(2)}, u32[]{:S(2)}) collective-permute-start(bf16[128,640]{1,0:T(8,128)(2,1)} %refs_0_.1), channel_id=1, source_target_pairs={{0,24},{8,16},{16,8},{24,0},{1,25},{9,17},{17,9},{25,1},{2,26},{10... | collective-permute-start | bytes 491528 | tf_op jit(solution)/shard_map/ppermute | solution.py:191
  4.6 3.8 %collective-permute-start.3 = (f32[32,16]{1,0:T(8,128)S(1)}, f32[32,16]{1,0:T(8,128)S(1)}, u32[]{:S(2)}, u32[]{:S(2)}) collective-permute-start(f32[32,16]{1,0:T(8,128)S(1)} %broadcast_select_fusion), channel_id=1, source_target_pairs={{0,1},{1,0},{2,3},{3,2},{4,5},{5,4},{6,7},{7,6},{8,9},{9,8},{10,11... | collective-permute-start | bytes 6152 | tf_op jit(solution)/shard_map/ppermute | solution.py:191
  9.1 8.1 %collective-permute-start.5 = (f32[32,16]{1,0:T(8,128)S(1)}, f32[32,16]{1,0:T(8,128)S(1)}, u32[]{:S(2)}, u32[]{:S(2)}) collective-permute-start(f32[32,16]{1,0:T(8,128)S(1)} %fusion.114), channel_id=1, source_target_pairs={{0,4},{1,5},{2,6},{3,7},{4,0},{5,1},{6,2},{7,3},{8,12},{9,13},{10,... | collective-permute-start | bytes 6152 | tf_op jit(solution)/shard_map/ppermute | solution.py:191
  12.1 5.5 %collective-permute-start.6 = (f32[32,16]{1,0:T(8,128)S(1)}, f32[32,16]{1,0:T(8,128)S(1)}, u32[]{:S(2)}, u32[]{:S(2)}) collective-permute-start(f32[32,16]{1,0:T(8,128)S(1)} %fusion.114), channel_id=1, source_target_pairs={{0,6},{1,7},{2,4},{3,5},{4,2},{5,3},{6,0},{7,1},{8,14},{9,15},{10,... | collective-permute-start | bytes 6152 | tf_op jit(solution)/shard_map/ppermute | solution.py:191
  13.5 4.2 %collective-permute-start.4 = (f32[32,16]{1,0:T(8,128)S(1)}, f32[32,16]{1,0:T(8,128)S(1)}, u32[]{:S(2)}, u32[]{:S(2)}) collective-permute-start(f32[32,16]{1,0:T(8,128)S(1)} %fusion.114), channel_id=1, source_target_pairs={{0,2},{1,3},{2,0},{3,1},{4,6},{5,7},{6,4},{7,5},{8,10},{9,11},{10,... | collective-permute-start | bytes 6152 | tf_op jit(solution)/shard_map/ppermute | solution.py:191
  17.3 8.3 %copy-start.2 = (bf16[512,640]{1,0:T(8,128)(2,1)}, bf16[512,640]{1,0:T(8,128)(2,1)S(1)}, u32[]{:S(2)}) copy-start(bf16[512,640]{1,0:T(8,128)(2,1)S(1)} %get-tuple-element.34) | copy-start | bytes 1966084
  18.4 14.8 %collective-permute-start.9 = (f32[32,16]{1,0:T(8,128)S(1)}, f32[32,16]{1,0:T(8,128)S(1)}, u32[]{:S(2)}, u32[]{:S(2)}) collective-permute-start(f32[32,16]{1,0:T(8,128)S(1)} %add_add_fusion.1), channel_id=1, source_target_pairs={{0,24},{8,16},{16,8},{24,0},{1,25},{9,17},{17,9},{25,1},{2,26},{10... | collective-permute-start | bytes 6152 | tf_op jit(solution)/shard_map/ppermute | solution.py:191
  18.4 14.8 %collective-permute-start.8 = (f32[32,16]{1,0:T(8,128)S(1)}, f32[32,16]{1,0:T(8,128)S(1)}, u32[]{:S(2)}, u32[]{:S(2)}) collective-permute-start(f32[32,16]{1,0:T(8,128)S(1)} %add_add_fusion.1), channel_id=1, source_target_pairs={{0,16},{8,24},{16,0},{24,8},{1,17},{9,25},{17,1},{25,9},{2,18},{10... | collective-permute-start | bytes 6152 | tf_op jit(solution)/shard_map/ppermute | solution.py:191
  19.9 13.2 %collective-permute-start.7 = (f32[32,16]{1,0:T(8,128)S(1)}, f32[32,16]{1,0:T(8,128)S(1)}, u32[]{:S(2)}, u32[]{:S(2)}) collective-permute-start(f32[32,16]{1,0:T(8,128)S(1)} %add_add_fusion.1), channel_id=1, source_target_pairs={{0,8},{8,0},{16,24},{24,16},{1,9},{9,1},{17,25},{25,17},{2,10},{10... | collective-permute-start | bytes 6152 | tf_op jit(solution)/shard_map/ppermute | solution.py:191
  20.4 7.8 %slice-start.2 = ((s8[4587520]{0:T(1024)(128)(4,1)}), s8[4194304]{0:T(1024)(128)(4,1)S(1)}, s32[]{:S(2)}) async-start(s8[4587520]{0:T(1024)(128)(4,1)} %bitcast.11), calls=%async_computation.2 | async-start | bytes 8388608
  20.7 7.5 %slice-start.3 = ((s8[4587520]{0:T(1024)(128)(4,1)}), s8[393216]{0:T(1024)(128)(4,1)S(1)}, s32[]{:S(2)}) async-start(s8[4587520]{0:T(1024)(128)(4,1)} %bitcast.11), calls=%async_computation.3 | async-start | bytes 786432
  26.2 26.8 %collective-permute-start.12 = (f16[256,1792]{1,0:T(8,128)(2,1)}, f16[256,1792]{1,0:T(8,128)(2,1)}, u32[]{:S(2)}, u32[]{:S(2)}) collective-permute-start(f16[256,1792]{1,0:T(8,128)(2,1)} %fusion.9), channel_id=1, source_target_pairs={{0,1},{1,0},{2,3},{3,2},{4,5},{5,4},{6,7},{7,6},{8,9},{9,8},{10,11... | collective-permute-start | bytes 2752520 | tf_op jit(solution)/shard_map/ppermute | solution.py:191
  28.2 21.4 %slice-start = ((s8[4587520]{0:T(1024)(128)(4,1)}), s8[393216]{0:T(1024)(128)(4,1)S(1)}, s32[]{:S(2)}) async-start(s8[4587520]{0:T(1024)(128)(4,1)} %bitcast.9), calls=%async_computation | async-start | bytes 786432
  31.7 28.7 %collective-permute-start.10 = (f16[256,1792]{1,0:T(8,128)(2,1)}, f16[256,1792]{1,0:T(8,128)(2,1)}, u32[]{:S(2)}, u32[]{:S(2)}) collective-permute-start(f16[256,1792]{1,0:T(8,128)(2,1)} %fusion.8), channel_id=1, source_target_pairs={{0,2},{1,3},{2,0},{3,1},{4,6},{5,7},{6,4},{7,5},{8,10},{9,11},{10,... | collective-permute-start | bytes 2752520 | tf_op jit(solution)/shard_map/ppermute | solution.py:191
  33.4 2.3 %copy-start = (bf16[640,3584]{1,0:T(8,128)(2,1)S(1)}, bf16[640,3584]{1,0:T(8,128)(2,1)}, u32[]{:S(2)}) copy-start(bf16[640,3584]{1,0:T(8,128)(2,1)} %refs_4_.6) | copy-start | bytes 13762564
  35.7 10.0 %copy-start.3 = (bf16[512,640]{1,0:T(8,128)(2,1)S(1)}, bf16[512,640]{1,0:T(8,128)(2,1)}, u32[]{:S(2)}) copy-start(bf16[512,640]{1,0:T(8,128)(2,1)} %copy-done.2) | copy-start | bytes 1966084
  35.7 13.9 %slice-start.1 = ((s8[4587520]{0:T(1024)(128)(4,1)}), s8[4194304]{0:T(1024)(128)(4,1)S(1)}, s32[]{:S(2)}) async-start(s8[4587520]{0:T(1024)(128)(4,1)} %bitcast.9), calls=%async_computation.1 | async-start | bytes 8388608
  49.1 36.8 %collective-permute-start.15 = (f16[256,1792]{1,0:T(8,128)(2,1)}, f16[256,1792]{1,0:T(8,128)(2,1)S(1)}, u32[]{:S(2)}, u32[]{:S(2)}) collective-permute-start(f16[256,1792]{1,0:T(8,128)(2,1)} %fusion.10), channel_id=1, source_target_pairs={{0,1},{1,0},{2,3},{3,2},{4,5},{5,4},{6,7},{7,6},{8,9},{9,8},{10,11... | collective-permute-start | bytes 2752520 | tf_op jit(solution)/shard_map/ppermute | solution.py:191
  55.6 18.8 %collective-permute-start.14 = (f16[128,1792]{1,0:T(8,128)(2,1)S(1)}, f16[128,1792]{1,0:T(8,128)(2,1)S(1)}, u32[]{:S(2)}, u32[]{:S(2)}) collective-permute-start(f16[128,1792]{1,0:T(8,128)(2,1)S(1)} %get-tuple-element.75), channel_id=1, source_target_pairs={{0,2},{1,3},{2,0},{3,1},{4,6},{5,7},{6,4},{7,5},{8,10},{9,11},{10,... | collective-permute-start | bytes 1376264 | tf_op jit(solution)/shard_map/ppermute | solution.py:191
  59.0 33.9 %collective-permute-start.17 = (f16[256,1792]{1,0:T(8,128)(2,1)}, f16[256,1792]{1,0:T(8,128)(2,1)S(1)}, u32[]{:S(2)}, u32[]{:S(2)}) collective-permute-start(f16[256,1792]{1,0:T(8,128)(2,1)} %fusion.11), channel_id=1, source_target_pairs={{0,2},{1,3},{2,0},{3,1},{4,6},{5,7},{6,4},{7,5},{8,10},{9,11},{10,... | collective-permute-start | bytes 2752520 | tf_op jit(solution)/shard_map/ppermute | solution.py:191
  62.5 18.6 %collective-permute-start.11 = (f16[128,1792]{1,0:T(8,128)(2,1)S(1)}, f16[128,1792]{1,0:T(8,128)(2,1)S(1)}, u32[]{:S(2)}, u32[]{:S(2)}) collective-permute-start(f16[128,1792]{1,0:T(8,128)(2,1)S(1)} %get-tuple-element.71), channel_id=1, source_target_pairs={{0,1},{1,0},{2,3},{3,2},{4,5},{5,4},{6,7},{7,6},{8,9},{9,8},{10,11... | collective-permute-start | bytes 1376264 | tf_op jit(solution)/shard_map/ppermute | solution.py:191
  81.8 39.2 %collective-permute-start.13 = (f16[64,1792]{1,0:T(8,128)(2,1)S(1)}, f16[64,1792]{1,0:T(8,128)(2,1)S(1)}, u32[]{:S(2)}, u32[]{:S(2)}) collective-permute-start(f16[64,1792]{1,0:T(8,128)(2,1)S(1)} %get-tuple-element.77), channel_id=1, source_target_pairs={{0,4},{1,5},{2,6},{3,7},{4,0},{5,1},{6,2},{7,3},{8,12},{9,13},{10,... | collective-permute-start | bytes 688136 | tf_op jit(solution)/shard_map/ppermute | solution.py:191
  83.5 37.5 %collective-permute-start.19 = (f16[64,1792]{1,0:T(8,128)(2,1)S(1)}, f16[64,1792]{1,0:T(8,128)(2,1)S(1)}, u32[]{:S(2)}, u32[]{:S(2)}) collective-permute-start(f16[64,1792]{1,0:T(8,128)(2,1)S(1)} %get-tuple-element.79), channel_id=1, source_target_pairs={{0,4},{1,5},{2,6},{3,7},{4,0},{5,1},{6,2},{7,3},{8,12},{9,13},{10,... | collective-permute-start | bytes 688136 | tf_op jit(solution)/shard_map/ppermute | solution.py:191
  86.1 20.7 %collective-permute-start.16 = (f16[128,1792]{1,0:T(8,128)(2,1)S(1)}, f16[128,1792]{1,0:T(8,128)(2,1)S(1)}, u32[]{:S(2)}, u32[]{:S(2)}) collective-permute-start(f16[128,1792]{1,0:T(8,128)(2,1)S(1)} %get-tuple-element.69), channel_id=1, source_target_pairs={{0,2},{1,3},{2,0},{3,1},{4,6},{5,7},{6,4},{7,5},{8,10},{9,11},{10,... | collective-permute-start | bytes 1376264 | tf_op jit(solution)/shard_map/ppermute | solution.py:191
  93.1 16.2 %collective-permute-start.18 = (f16[128,1792]{1,0:T(8,128)(2,1)S(1)}, f16[128,1792]{1,0:T(8,128)(2,1)S(1)}, u32[]{:S(2)}, u32[]{:S(2)}) collective-permute-start(f16[128,1792]{1,0:T(8,128)(2,1)S(1)} %get-tuple-element.73), channel_id=1, source_target_pairs={{0,1},{1,0},{2,3},{3,2},{4,5},{5,4},{6,7},{7,6},{8,9},{9,8},{10,11... | collective-permute-start | bytes 1376264 | tf_op jit(solution)/shard_map/ppermute | solution.py:191
  107.5 16.9 %collective-permute-start.20 = (f16[64,1792]{1,0:T(8,128)(2,1)S(1)}, f16[64,1792]{1,0:T(8,128)(2,1)S(1)}, u32[]{:S(2)}, u32[]{:S(2)}) collective-permute-start(f16[64,1792]{1,0:T(8,128)(2,1)S(1)} %get-tuple-element.81), channel_id=1, source_target_pairs={{0,4},{1,5},{2,6},{3,7},{4,0},{5,1},{6,2},{7,3},{8,12},{9,13},{10,... | collective-permute-start | bytes 688136 | tf_op jit(solution)/shard_map/ppermute | solution.py:191
  110.1 19.1 %collective-permute-start.21 = (f16[64,1792]{1,0:T(8,128)(2,1)S(1)}, f16[64,1792]{1,0:T(8,128)(2,1)S(1)}, u32[]{:S(2)}, u32[]{:S(2)}) collective-permute-start(f16[64,1792]{1,0:T(8,128)(2,1)S(1)} %get-tuple-element.83), channel_id=1, source_target_pairs={{0,4},{1,5},{2,6},{3,7},{4,0},{5,1},{6,2},{7,3},{8,12},{9,13},{10,... | collective-permute-start | bytes 688136 | tf_op jit(solution)/shard_map/ppermute | solution.py:191
